TPU v7x, 32 devices: a whole 2x2x4 slice. The times are simulated.
32 devices in a mesh: blk: 8 (over y, x, core), uly: 4 (over z).
Axes of the slice: x: 2, y: 2, z: 4, core: 2. Of those that a mesh axis runs over, the one named last changes fastest.
Arguments:
- hidden_in: bfloat16 [2048, 3072], P(('blk', 'uly')), may hold values from -6 to 6
- cached_out: bfloat16 [2048, 3072], P(('blk', 'uly')), may hold values from -6 to 6
- cache_keys: bfloat16 [2048, 3072], P(('blk', 'uly')), may hold values from -288 to 288
- cache_values: bfloat16 [2048, 3072], P(('blk', 'uly')), may hold values from -36 to 36
- refresh_idx: int32 [512], P(('blk', 'uly')), may hold values from -1 to 63, as said below
- modulation: float32 [6, 3072], replicated, may hold values from -3 to 3
- q_gain: float32 [128], replicated, may hold values from 1.5 to 4
- w_query: bfloat16 [3072, 3072], P(None, 'uly'), may hold values from -0.109375 to 0.109375
- w_out: bfloat16 [3072, 3072], P('uly'), may hold values from -0.109375 to 0.109375
- w_up: bfloat16 [3072, 12288], P(None, 'blk'), may hold values from -0.109375 to 0.109375
- w_down: bfloat16 [12288, 3072], P('blk'), may hold values from -0.0546875 to 0.0546875
Outputs:
- features: bfloat16 [2048, 3072], P(('blk', 'uly'))
Inputs may be any that keep to these rules, and one draw needn't show every extreme that they name: `refresh_idx`: each device's 16 slots name distinct positions among that device's own 64 positions, live slots first and -1 in the rest. Among the devices that share a blk index, one has all 16 slots live and every other at most 8; so such a group has at most 40 live slots, and some group has exactly 40.
All inputs are finite; a program needn't handle non-finite values.
Results may differ from a plain program's by a relative error of at most 0.023.
The roundings to bfloat16 on the way count: a program that leaves them out, or rounds other values in their place, can miss the bound.
Values may be sent and summed in bfloat16 or wider, within the bound.
No kernel may reach another device: no remote copies, remote signals or barrier semaphores. Data moves between devices by JAX's collectives and lax.ppermute only.
A program may use at most 128 MiB of HBM per device.

v0:
```python
import functools
import math

import jax
import jax.numpy as jnp
from jax import lax
from jax.experimental import pallas as pl
from jax.experimental.pallas import tpu as pltpu
from jax.sharding import PartitionSpec as P

DH = 128
OTHER = 8
VMEM_SPEC = pl.BlockSpec(memory_space=pltpu.VMEM)
TOKEN = jax.ShapeDtypeStruct((8, DH), jnp.float32)
ANY_SPEC = pl.BlockSpec(memory_space=pl.ANY)


def double(x, axis, scale, count, on_arrival=()):
    have = {0: x}
    for k in sorted(range(1, count), key=lambda k: (bin(k).count("1"), -k)):
        low = k & -k
        have[k] = trade(have[k ^ low], axis, low * scale)
        if k in on_arrival:
            have[k] = on_arrival[k](have[k])
    return [have[k] for k in range(count)]


def layer_norm(row_block, shift_by, scale_by):
    average = jnp.mean(row_block, axis=-1, keepdims=True)
    centred = row_block - average
    spread = jnp.mean(centred * centred, axis=-1, keepdims=True)
    return centred * lax.rsqrt(spread + 1e-06) * (1.0 + scale_by) + shift_by


def trade(x, axis, flip):
    if flip == 0:
        return x
    return lax.ppermute(x, axis, [(i, i ^ flip) for i in range(lax.axis_size(axis))])


def in_hbm(x):
    return pltpu.with_memory_space_constraint(x, pltpu.HBM)


def hold_kernel(count, *refs):
    source_refs, sems = refs[1 : count + 1], refs[-1]
    *held_refs, token_ref = refs[count + 1 : -1]
    token_ref[...] = jnp.zeros_like(token_ref)
    copies = [
        pltpu.make_async_copy(source_ref, held_ref, sems.at[i])
        for i, (source_ref, held_ref) in enumerate(zip(source_refs, held_refs))
    ]
    for copy in copies:
        copy.start()
    for copy in copies:
        copy.wait()


def hold(after, *weights):
    count = len(weights)
    moved = sum(w.size * w.dtype.itemsize for w in weights)
    return pl.pallas_call(
        functools.partial(hold_kernel, count),
        in_specs=[VMEM_SPEC] + [ANY_SPEC] * count,
        out_specs=[VMEM_SPEC] * (count + 1),
        out_shape=[pltpu.VMEM(w.shape, w.dtype) for w in weights] + [TOKEN],
        scratch_shapes=[pltpu.SemaphoreType.DMA((count,))],
        cost_estimate=pl.CostEstimate(flops=0, bytes_accessed=moved, transcendentals=0),
        compiler_params=pltpu.CompilerParams(vmem_limit_bytes=2 << 20),
        name="hold",
    )(after, *[in_hbm(w) for w in weights])


def my_core(pair):
    return lax.rem(lax.axis_index("blk"), pair)


def enter_kernel(pair, idx_hbm, hidden_hbm, mod_hbm, key_hbm, value_hbm, *refs):
    rows_ref, normed_ref, select_ref, mod_ref, *side_refs = refs[: pair + 4]
    idx_ref, hidden_ref, sems, kv_sem = refs[pair + 4 :]
    copies = [
        pltpu.make_async_copy(source, target, sems.at[i])
        for i, (source, target) in enumerate(
            [(idx_hbm, idx_ref), (hidden_hbm, hidden_ref), (mod_hbm, mod_ref)]
        )
    ]
    for copy in copies:
        copy.start()
    parts, _, both = side_refs[0].shape
    half = both // 2
    uly, core = lax.axis_index("uly"), my_core(pair)
    kv_copies = []
    for side, side_ref in enumerate(side_refs):
        for flip in range(parts):
            start = pl.multiple_of(((uly ^ flip) * pair + (core ^ side)) * half, DH)
            for at, source in enumerate((key_hbm, value_hbm)):
                copy = pltpu.make_async_copy(
                    source.at[:, pl.ds(start, half)],
                    side_ref.at[flip, :, pl.ds(at * half, half)],
                    kv_sem.at[side, flip, at],
                )
                copy.start()
                kv_copies.append(copy)
    for copy in copies:
        copy.wait()
    tokens, width = hidden_ref.shape
    slots = idx_ref.shape[1]
    position = lax.broadcasted_iota(jnp.int32, (tokens, slots), 0)
    select = (position == idx_ref[...]).astype(jnp.float32).astype(jnp.bfloat16)
    select_ref[...] = select
    contract = (((0,), (0,)), ((), ()))
    rows = lax.dot_general(
        select, hidden_ref[...], contract, preferred_element_type=jnp.float32
    )
    live = lax.dot_general(
        select,
        jnp.ones((tokens, DH), jnp.bfloat16),
        contract,
        preferred_element_type=jnp.float32,
    )
    rows_ref[...] = rows
    normed = layer_norm(rows, mod_ref[0:1, :], mod_ref[1:2, :])
    normed_ref[:, :width] = normed.astype(jnp.bfloat16)
    normed_ref[:, width:] = live.astype(jnp.bfloat16)
    for copy in kv_copies:
        copy.wait()


def enter(refresh_idx, hidden_in, modulation, cache_keys, cache_values, parts, pair):
    slots = refresh_idx.shape[0]
    tokens, width = hidden_in.shape
    both = 2 * width // (parts * pair)
    out = pl.pallas_call(
        functools.partial(enter_kernel, pair),
        in_specs=[ANY_SPEC] * 5,
        out_specs=[VMEM_SPEC] * (pair + 4),
        out_shape=[
            pltpu.VMEM((slots, width), jnp.float32),
            pltpu.VMEM((slots, width + DH), jnp.bfloat16),
            pltpu.VMEM((tokens, slots), jnp.bfloat16),
            pltpu.VMEM(modulation.shape, modulation.dtype),
        ]
        + [pltpu.VMEM((parts, tokens, both), cache_keys.dtype)] * pair,
        scratch_shapes=[
            pltpu.VMEM((1, slots), jnp.int32),
            pltpu.VMEM(hidden_in.shape, hidden_in.dtype),
            pltpu.SemaphoreType.DMA((3,)),
            pltpu.SemaphoreType.DMA((pair, parts, 2)),
        ],
        compiler_params=pltpu.CompilerParams(vmem_limit_bytes=8 << 20),
        name="enter",
    )(
        *[
            in_hbm(x)
            for x in (refresh_idx.reshape(1, slots), hidden_in, modulation, cache_keys, cache_values)
        ]
    )
    return *out[:4], out[4:]


def merge_kv_kernel(sides, flips, *refs):
    *refs, token_ref = refs
    token_ref[...] = jnp.zeros_like(token_ref)
    for flip, out_ref in zip(flips, refs[-len(flips) :]):
        for side in range(sides):
            out_ref[side] = refs[side][flip]


def merge_kv(sides, flips, after):
    _, tokens, both = sides[0].shape
    *merged, token = pl.pallas_call(
        functools.partial(merge_kv_kernel, len(sides), flips),
        out_specs=[VMEM_SPEC] * (len(flips) + 1),
        out_shape=[pltpu.VMEM((len(sides), tokens, both), sides[0].dtype) for _ in flips]
        + [TOKEN],
        compiler_params=pltpu.CompilerParams(vmem_limit_bytes=8 << 20),
        name="merge_kv",
    )(*sides, *after)
    return merged, token


def relay_kernel(x_ref, after_ref, out_ref):
    out_ref[...] = x_ref[...]


def relay(x, after):
    return pl.pallas_call(
        relay_kernel,
        out_specs=VMEM_SPEC,
        out_shape=pltpu.VMEM(x.shape, x.dtype),
        compiler_params=pltpu.CompilerParams(vmem_limit_bytes=2 << 20),
        name="relay",
    )(x, after)


def project_kernel(pieces, after_ref, *refs):
    rows_refs, (w_ref, gain_hbm_ref) = refs[:pieces], refs[pieces : pieces + 2]
    *query_refs, spread_ref, token_ref, heads_ref, gain_ref, sem = refs[pieces + 2 :]
    token_ref[...] = jnp.zeros_like(token_ref)
    copy = pltpu.make_async_copy(gain_hbm_ref, gain_ref, sem)
    copy.start()
    core = my_core(len(query_refs))
    width = w_ref.shape[0]
    group, half = query_refs[0].shape
    rows = jnp.concatenate([ref[...] for ref in rows_refs], axis=0)
    everyone = rows.shape[0]
    flags = rows[:, width:]
    shape = (everyone, everyone)
    before = lax.broadcasted_iota(jnp.int32, shape, 1) < lax.broadcasted_iota(jnp.int32, shape, 0)
    before = before.astype(jnp.float32).astype(jnp.bfloat16)
    rank = jnp.dot(before, flags, preferred_element_type=jnp.float32)
    lane = lax.broadcasted_iota(jnp.int32, rank.shape, 1).astype(jnp.float32)
    spread = jnp.where((rank == lane) & (flags.astype(jnp.float32) > 0.0), 1.0, 0.0)
    spread = spread.astype(jnp.bfloat16)
    spread_ref[...] = spread
    live_rows = lax.dot_general(
        spread[:, :group],
        rows[:, :width],
        (((0,), (0,)), ((), ())),
        preferred_element_type=jnp.float32,
    ).astype(jnp.bfloat16)
    projected = jnp.dot(live_rows, w_ref[...], preferred_element_type=jnp.float32)
    copy.wait()
    for start in range(0, projected.shape[1], DH):
        head = projected[:, start : start + DH]
        squares = jnp.mean(head * head, axis=-1, keepdims=True)
        heads_ref[:, start : start + DH] = (
            head * lax.rsqrt(squares + 1e-06) * (gain_ref[...] / math.sqrt(DH))
        )
    for side, query_ref in enumerate(query_refs):
        start = pl.multiple_of((core ^ side) * half, DH)
        query_ref[...] = heads_ref[:, pl.ds(start, half)].astype(jnp.bfloat16)


def project(after, rows, w_query, q_gain, group, pair):
    half = w_query.shape[1] // pair
    everyone = len(rows) * rows[0].shape[0]
    query = jax.ShapeDtypeStruct((group, half), jnp.bfloat16)
    out = pl.pallas_call(
        functools.partial(project_kernel, len(rows)),
        in_specs=[VMEM_SPEC] * (len(rows) + 2) + [ANY_SPEC],
        out_shape=[query] * pair + [jax.ShapeDtypeStruct((everyone, DH), jnp.bfloat16), TOKEN],
        scratch_shapes=[
            pltpu.VMEM((group, w_query.shape[1]), jnp.float32),
            pltpu.VMEM((1, DH), jnp.float32),
            pltpu.SemaphoreType.DMA,
        ],
        compiler_params=pltpu.CompilerParams(vmem_limit_bytes=16 << 20),
        name="project",
    )(after, *rows, w_query, in_hbm(q_gain.reshape(1, DH)))
    return out[:-2], out[-2], out[-1]


def attend_kernel(pieces, after_ref, *refs):
    *refs, token_ref = refs
    token_ref[...] = jnp.zeros_like(token_ref)
    query_refs, kv_refs, out_refs = refs[:pieces], refs[pieces:-pieces], refs[-pieces:]
    cores, group, half = query_refs[0].shape
    rows = cores * group
    sides = kv_refs[0].shape[0]
    lane = lax.broadcasted_iota(jnp.int32, (DH, DH), 1)
    for at in range(0, pieces, 4):
        stop = min(at + 4, pieces)
        queries = [ref[core] for ref in query_refs[at:stop] for core in range(cores)]
        queries = [x.astype(jnp.float32) for x in queries]
        queries = jnp.concatenate(queries, axis=0).astype(jnp.bfloat16)
        stats = [jnp.zeros((DH, DH), jnp.float32) for _ in range(at, stop)]
        for head in range(half // DH):
            cols = slice(head * DH, (head + 1) * DH)
            vals = slice(half + head * DH, half + (head + 1) * DH)
            keys = [ref[side, :, cols] for ref in kv_refs for side in range(sides)]
            values = [ref[side, :, vals] for ref in kv_refs for side in range(sides)]
            scores = lax.dot_general(
                queries[:, cols],
                jnp.concatenate(keys, axis=0),
                (((1,), (1,)), ((), ())),
                preferred_element_type=jnp.float32,
            )
            maxima = jnp.max(scores, axis=-1, keepdims=True)
            weights = jnp.exp(scores - maxima)
            sums = jnp.sum(weights, axis=-1, keepdims=True)
            weighted = jnp.dot(
                weights.astype(jnp.bfloat16),
                jnp.concatenate(values, axis=0),
                preferred_element_type=jnp.float32,
            )
            for j in range(at, stop):
                mine = slice((j - at) * rows, (j - at + 1) * rows)
                out_refs[j][:rows, cols] = weighted[mine]
                pad = jnp.zeros((DH - rows, 1), jnp.float32)
                top = jnp.concatenate([maxima[mine], pad], axis=0)
                total = jnp.concatenate([sums[mine], pad], axis=0)
                stat = jnp.where(lane == 2 * head, top, stats[j - at])
                stats[j - at] = jnp.where(lane == 2 * head + 1, total, stat)
        for j in range(at, stop):
            out_refs[j][rows:, DH:] = jnp.zeros((8, half - DH), jnp.float32)
            out_refs[j][rows:, :DH] = stats[j - at].T[:8]


def attend(after, queries, kv_parts):
    cores, group, half = queries[0].shape
    rows = cores * group
    return pl.pallas_call(
        functools.partial(attend_kernel, len(queries)),
        out_shape=[jax.ShapeDtypeStruct((rows + 8, half), jnp.float32)] * len(queries) + [TOKEN],
        compiler_params=pltpu.CompilerParams(vmem_limit_bytes=24 << 20),
        name="attend",
    )(after, *queries, *kv_parts)


def combine_kernel(pieces, after_ref, *refs):
    part_refs, out_refs = refs[:pieces], refs[pieces:]
    group, half = out_refs[0].shape
    rows = group * len(out_refs)
    stats = []
    for ref in part_refs:
        packed = ref[rows:, :DH]
        packed = jnp.concatenate([packed, jnp.zeros((DH - 8, DH), jnp.float32)], axis=0)
        stats.append(packed.T[:rows])
    for head in range(half // DH):
        cols = slice(head * DH, (head + 1) * DH)
        maxima = [stat[:, 2 * head : 2 * head + 1] for stat in stats]
        top = functools.reduce(jnp.maximum, maxima)
        total = jnp.zeros_like(top)
        attended = jnp.zeros((rows, DH), jnp.float32)
        for ref, stat, maximum in zip(part_refs, stats, maxima):
            factor = jnp.exp(maximum - top)
            total = total + stat[:, 2 * head + 1 : 2 * head + 2] * factor
            attended = attended + ref[:rows, cols] * factor
        attended = attended / total
        for side, out_ref in enumerate(out_refs):
            out_ref[:, cols] = attended[side * group : (side + 1) * group].astype(jnp.bfloat16)


def combine(after, parts, group, pair):
    half = parts[0].shape[1]
    return pl.pallas_call(
        functools.partial(combine_kernel, len(parts)),
        out_shape=[jax.ShapeDtypeStruct((group, half), jnp.bfloat16)] * pair,
        compiler_params=pltpu.CompilerParams(vmem_limit_bytes=16 << 20),
        name="combine",
    )(after, *parts)


def output_kernel(sides, spread_ref, *refs):
    side_refs, w_ref, (*out_refs, token_ref) = refs[:sides], refs[sides], refs[sides + 1 :]
    token_ref[...] = jnp.zeros_like(token_ref)
    group, half = side_refs[0].shape
    slots, width = out_refs[0].shape
    spread = spread_ref[:, :group]
    attended = [
        jnp.dot(spread, ref[...], preferred_element_type=jnp.float32).astype(jnp.bfloat16)
        for ref in side_refs
    ]
    core = my_core(sides)
    starts = [pl.multiple_of((core ^ side) * half, DH) for side in range(sides)]
    step = math.gcd(width, 1024)
    for col in range(0, width, step):
        terms = jnp.zeros((spread.shape[0], step), jnp.float32)
        for start, side in zip(starts, attended):
            terms = terms + jnp.dot(
                side, w_ref[pl.ds(start, half), col : col + step], preferred_element_type=jnp.float32
            )
        for k, out_ref in enumerate(out_refs):
            piece = terms[k * slots : (k + 1) * slots]
            out_ref[:, col : col + step] = piece.astype(out_ref.dtype)


def output(spread, sides, w_out, slots, parts):
    width = w_out.shape[1]
    return pl.pallas_call(
        functools.partial(output_kernel, len(sides)),
        out_shape=[
            jax.ShapeDtypeStruct((slots, width), jnp.bfloat16 if k else jnp.float32)
            for k in range(parts)
        ]
        + [TOKEN],
        compiler_params=pltpu.CompilerParams(vmem_limit_bytes=16 << 20),
        name="output",
    )(spread, *sides, w_out)


def mlp_kernel(pieces, *refs):
    row_refs, (up_ref, down_ref) = refs[:pieces], refs[pieces : pieces + 2]
    *out_refs, act_ref = refs[pieces + 2 :]
    hidden, width = down_ref.shape
    rows = [ref[j] for ref in row_refs for j in range(ref.shape[0])]
    rows = jnp.concatenate(rows, axis=0)
    count = out_refs[0].shape[0]
    step = math.gcd(hidden, 512)
    for col in range(0, hidden, step):
        lifted = jnp.dot(rows, up_ref[:, col : col + step], preferred_element_type=jnp.float32)
        act_ref[:, col : col + step] = jax.nn.gelu(lifted, approximate=True).astype(jnp.bfloat16)
    step = math.gcd(width, 512)
    for col in range(0, width, step):
        down = jnp.dot(
            act_ref[...], down_ref[:, col : col + step], preferred_element_type=jnp.float32
        )
        for side, out_ref in enumerate(out_refs):
            piece = down[side * count : (side + 1) * count]
            out_ref[:, col : col + step] = piece.astype(out_ref.dtype)


def mlp(rows, w_up, w_down, pair):
    count = sum(x.shape[0] * x.shape[1] for x in rows)
    hidden, width = w_down.shape
    return pl.pallas_call(
        functools.partial(mlp_kernel, len(rows)),
        out_shape=[
            jax.ShapeDtypeStruct((count // pair, width), jnp.bfloat16 if side else jnp.float32)
            for side in range(pair)
        ],
        scratch_shapes=[pltpu.VMEM((count, hidden), jnp.bfloat16)],
        compiler_params=pltpu.CompilerParams(vmem_limit_bytes=32 << 20),
        name="mlp",
    )(*rows, w_up, w_down)


def join_kernel(count, *refs):
    part_refs, out_ref = refs[:count], refs[-1]
    for at, ref in enumerate(part_refs):
        out_ref[at] = ref[...]


def join(parts, after=()):
    return pl.pallas_call(
        functools.partial(join_kernel, len(parts)),
        out_shape=jax.ShapeDtypeStruct((len(parts), *parts[0].shape), parts[0].dtype),
        compiler_params=pltpu.CompilerParams(vmem_limit_bytes=8 << 20),
        name="join",
    )(*parts, *after)


def renorm_kernel(hold_ref, rows_ref, mod_ref, *refs):
    *term_refs, after_ref, normed_ref = refs
    branch = term_refs[0][...]
    for ref in term_refs[1:]:
        branch = branch + ref[...].astype(jnp.float32)
    after = rows_ref[...] + mod_ref[2:3, :] * branch
    after_ref[...] = after
    normed_ref[...] = layer_norm(after, mod_ref[3:4, :], mod_ref[4:5, :]).astype(jnp.bfloat16)


def renorm(after, rows_in, modulation, terms):
    return pl.pallas_call(
        renorm_kernel,
        out_shape=[
            jax.ShapeDtypeStruct(rows_in.shape, jnp.float32),
            jax.ShapeDtypeStruct(rows_in.shape, jnp.bfloat16),
        ],
        compiler_params=pltpu.CompilerParams(vmem_limit_bytes=8 << 20),
        name="renorm",
    )(after, rows_in, modulation, *terms)


def fold_kernel(sides, *refs):
    side_refs, out_refs = refs[:sides], refs[sides:]
    slots = out_refs[0].shape[0]
    for j, out_ref in enumerate(out_refs):
        total = side_refs[0][j * slots : (j + 1) * slots]
        for ref in side_refs[1:]:
            total = total + ref[j * slots : (j + 1) * slots].astype(jnp.float32)
        out_ref[...] = total.astype(out_ref.dtype)


def fold(sides, slots):
    count, width = sides[0].shape
    return pl.pallas_call(
        functools.partial(fold_kernel, len(sides)),
        out_shape=[
            jax.ShapeDtypeStruct((slots, width), jnp.bfloat16 if j else jnp.float32)
            for j in range(count // slots)
        ],
        compiler_params=pltpu.CompilerParams(vmem_limit_bytes=8 << 20),
        name="fold",
    )(*sides)


def finish_kernel(select_ref, cached_ref, after_ref, mod_ref, *refs):
    *term_refs, out_ref = refs
    total = term_refs[0][...]
    for ref in term_refs[1:]:
        total = total + ref[...].astype(jnp.float32)
    renewed = (after_ref[...] + mod_ref[5:6, :] * total).astype(jnp.bfloat16)
    select = select_ref[...]
    placed = jnp.dot(select, renewed, preferred_element_type=jnp.float32)
    covered = jnp.sum(select.astype(jnp.float32), axis=1, keepdims=True)
    blended = cached_ref[...].astype(jnp.float32) * (1.0 - covered) + placed
    out_ref[...] = blended.astype(jnp.bfloat16)


def finish(select, cached, after_attn, modulation, terms):
    return pl.pallas_call(
        finish_kernel,
        out_shape=jax.ShapeDtypeStruct(cached.shape, jnp.bfloat16),
        compiler_params=pltpu.CompilerParams(vmem_limit_bytes=8 << 20),
        name="finish",
    )(select, cached, after_attn, modulation, *terms)


def body(
    hidden_in,
    cached_out,
    cache_keys,
    cache_values,
    refresh_idx,
    modulation,
    q_gain,
    w_query,
    w_out,
    w_up,
    w_down,
):
    slots = refresh_idx.shape[0]
    uly_size = lax.axis_size("uly")
    blk_size = lax.axis_size("blk")
    local_heads = w_query.shape[1] // DH
    group = min(slots * uly_size, slots + (uly_size - 1) * OTHER)
    pair = 2 if blk_size % 2 == 0 and local_heads % 2 == 0 else 1
    chips = blk_size // pair

    rows_in, normed, select, modulation, sides = enter(
        refresh_idx, hidden_in, modulation, cache_keys, cache_values, uly_size, pair
    )
    sides = [trade(x, "blk", side) for side, x in enumerate(sides)]
    w_query, token = hold(normed, w_query)
    half_way = uly_size // 2
    group_rows = double(normed, "uly", 1, uly_size, {half_way: lambda x: relay(x, token)})
    cuts = [[half_way], [k for k in reversed(range(uly_size)) if k not in (1, half_way)]]
    first, token = merge_kv(sides, cuts[0], [group_rows[half_way]])
    second, token = merge_kv(sides, cuts[1], [token] + group_rows[1:])
    kv_parts = [trade(x, "uly", k) for k, x in zip(cuts[0] + cuts[1], first + second)]

    queries, spread, token = project(token, group_rows, w_query, q_gain, group, pair)
    last, _ = merge_kv(sides, [1], [token])
    kv_parts.append(trade(last[0], "uly", 1))
    w_out, token = hold(token, w_out)
    queries = join([trade(x, "blk", side) for side, x in enumerate(queries)])
    queries = double(queries, "blk", pair, chips)
    *parts, token = attend(token, queries, kv_parts)
    w_up, token = hold(token, w_up)
    parts = [trade(x, "blk", j * pair) for j, x in enumerate(parts)]
    attended = combine(token, parts, group, pair)
    attended = [trade(x, "blk", side) for side, x in enumerate(attended)]
    *terms, token = output(spread, attended, w_out, slots, uly_size)
    w_down, cached, token = hold(token, w_down, cached_out)
    terms = [trade(x, "uly", k) for k, x in enumerate(terms)]
    after_attn, norm_mlp = renorm(token, rows_in, modulation, terms)

    rows = [join([trade(norm_mlp, "blk", j * pair) for j in range(chips)])]
    if pair == 2:
        rows.append(trade(rows[0], "blk", 1))
    down = mlp(rows, w_up, w_down, pair)
    down = [trade(x, "blk", side) for side, x in enumerate(down)]
    terms = [trade(x, "blk", j * pair) for j, x in enumerate(fold(down, slots))]
    return finish(select, cached, after_attn, modulation, terms)


def solution(mesh):
    return jax.shard_map(
        body,
        mesh=mesh,
        in_specs=(
            P(("blk", "uly"), None),
            P(("blk", "uly"), None),
            P(("blk", "uly"), None),
            P(("blk", "uly"), None),
            P(("blk", "uly")),
            P(),
            P(),
            P(None, "uly"),
            P("uly", None),
            P(None, "blk"),
            P("blk", None),
        ),
        out_specs=P(("blk", "uly"), None),
        check_vma=False,
    )
```

profile of v0, /device:TPU:0, one launch (start us, length us, event | category | flops | bytes accessed | tf_op | source)
XLA Modules:
  0.0 83.3 jit_solution(5984013099200454017)
XLA Ops:
  0.0 2.0 %enter.1 = (f32[16,3072]{1,0:T(8,128)S(1)}, bf16[16,3200]{1,0:T(8,128)(2,1)S(1)}, bf16[64,16]{1,0:T(8,128)(2,1)S(1)}, f32[6,3072]{1,0:T(8,128)S(1)}, bf16[4,64,7...) custom-call(s32[1,16]{1,0:T(1,128)} %bitcast.2, bf16[64,3072]{1,0:T(8,128)(2,1)} %hidden_hbm.1, f32[6,3072]{1,0:T(8,128)} %mod_hbm.1, ...), custom_call_target="tpu_custom_call" | custom-call | tf_op jit(solution)/shard_map/enter/pallas_call | solution.py:133
  2.6 3.7 %collective-permute-start.1 = (bf16[16,3200]{1,0:T(8,128)(2,1)S(1)}, bf16[16,3200]{1,0:T(8,128)(2,1)S(1)}, u32[]{:S(2)}, u32[]{:S(2)}) collective-permute-start(bf16[16,3200]{1,0:T(8,128)(2,1)S(1)} %get-tuple-element.53.refs_0_), channel_id=1, source_target_pairs={{0,2},{1,3},{2,0},{3,1},{4,6},{5,7},{6,4},{7,5},{8,10},{9,11},{10,... | collective-permute-start | bytes 307208 | tf_op jit(solution)/shard_map/ppermute | solution.py:38
  6.2 1.6 %collective-permute-start.2 = (bf16[16,3200]{1,0:T(8,128)(2,1)S(1)}, bf16[16,3200]{1,0:T(8,128)(2,1)S(1)}, u32[]{:S(2)}, u32[]{:S(2)}) collective-permute-start(bf16[16,3200]{1,0:T(8,128)(2,1)S(1)} %get-tuple-element.53.refs_0_), channel_id=1, source_target_pairs={{0,1},{1,0},{2,3},{3,2},{4,5},{5,4},{6,7},{7,6},{8,9},{9,8},{10,11... | collective-permute-start | bytes 307208 | tf_op jit(solution)/shard_map/ppermute | solution.py:38
  7.8 2.3 %hold.4 = (bf16[3072,768]{1,0:T(8,128)(2,1)S(1)}, f32[8,128]{1,0:T(8,128)S(1)}) custom-call(bf16[16,3200]{1,0:T(8,128)(2,1)S(1)} %get-tuple-element.53.refs_0_, bf16[3072,768]{1,0:T(8,128)(2,1)} %refs_1_.4), custom_call_target="tpu_custom_call" | custom-call | bytes 4718592 | tf_op jit(solution)/shard_map/hold/pallas_call | solution.py:62
  10.1 1.8 %collective-permute-done.1.x_ref = bf16[16,3200]{1,0:T(8,128)(2,1)S(1)} collective-permute-done((bf16[16,3200]{1,0:T(8,128)(2,1)S(1)}, bf16[16,3200]{1,0:T(8,128)(2,1)S(1)}, u32[]{:S(2)}, u32[]{:S(2)}) %collective-permute-start.1) | collective-permute-done | bytes 102432 | tf_op jit(solution)/shard_map/ppermute | solution.py:38
  12.7 3.4 %collective-permute-start.8 = (bf16[2,64,768]{2,1,0:T(8,128)(2,1)S(1)}, bf16[2,64,768]{2,1,0:T(8,128)(2,1)S(1)}, u32[]{:S(2)}, u32[]{:S(2)}) collective-permute-start(bf16[2,64,768]{2,1,0:T(8,128)(2,1)S(1)} %get-tuple-element.63), channel_id=1, source_target_pairs={{0,2},{1,3},{2,0},{3,1},{4,6},{5,7},{6,4},{7,5},{8,10},{9,11},{10,... | collective-permute-start | bytes 589832 | tf_op jit(solution)/shard_map/ppermute | solution.py:38
  19.6 4.0 %collective-permute-start.9 = (bf16[2,64,768]{2,1,0:T(8,128)(2,1)S(1)}, bf16[2,64,768]{2,1,0:T(8,128)(2,1)S(1)}, u32[]{:S(2)}, u32[]{:S(2)}) collective-permute-start(bf16[2,64,768]{2,1,0:T(8,128)(2,1)S(1)} %get-tuple-element.64), channel_id=1, source_target_pairs={{0,3},{1,2},{2,1},{3,0},{4,7},{5,6},{6,5},{7,4},{8,11},{9,10},{10,... | collective-permute-start | bytes 589832 | tf_op jit(solution)/shard_map/ppermute | solution.py:38
  24.8 1.5 %collective-permute-start.6 = (bf16[2,40,384]{2,1,0:T(8,128)(2,1)S(1)}, bf16[2,40,384]{2,1,0:T(8,128)(2,1)S(1)}, u32[]{:S(2)}, u32[]{:S(2)}) collective-permute-start(bf16[2,40,384]{2,1,0:T(8,128)(2,1)S(1)} %join.2.refs_0_), channel_id=1, source_target_pairs={{0,16},{4,20},{8,24},{12,28},{16,0},{20,4},{24,8},{28,12},{1,17},{... | collective-permute-start | bytes 184328 | tf_op jit(solution)/shard_map/ppermute | solution.py:38
  30.6 2.3 %hold.5 = (bf16[768,3072]{1,0:T(8,128)(2,1)S(1)}, f32[8,128]{1,0:T(8,128)S(1)}) custom-call(f32[8,128]{1,0:T(8,128)S(1)} %get-tuple-element.59.refs_0_.refs_2_, bf16[768,3072]{1,0:T(8,128)(2,1)} %refs_1_.5), custom_call_target="tpu_custom_call" | custom-call | bytes 4718592 | tf_op jit(solution)/shard_map/hold/pallas_call | solution.py:62
  33.3 3.2 %attend.1 = (f32[88,384]{1,0:T(8,128)S(1)}, f32[88,384]{1,0:T(8,128)S(1)}, f32[88,384]{1,0:T(8,128)S(1)}, f32[88,384]{1,0:T(8,128)S(1)}, f32[8,128]{1,0:T(8,128)S(1)}) custom-call(f32[8,128]{1,0:T(8,128)S(1)} %get-tuple-element.60.after_ref, bf16[2,40,384]{2,1,0:T(8,128)(2,1)S(1)} %join.2.refs_0_, bf16[2,40,384]{2,1,0:T(8,128)(2,1)S(1)} %collective-permute-done.5.refs_1_, ...), custom_call_target="tpu_custom_call" | custom-call | tf_op jit(solution)/shard_map/attend/pallas_call | solution.py:303
  38.1 1.5 %collective-permute-start.12 = (f32[88,384]{1,0:T(8,128)S(1)}, f32[88,384]{1,0:T(8,128)S(1)}, u32[]{:S(2)}, u32[]{:S(2)}) collective-permute-start(f32[88,384]{1,0:T(8,128)S(1)} %get-tuple-element.71), channel_id=1, source_target_pairs={{0,16},{4,20},{8,24},{12,28},{16,0},{20,4},{24,8},{28,12},{1,17},{... | collective-permute-start | bytes 405512 | tf_op jit(solution)/shard_map/ppermute | solution.py:38
  40.0 3.7 %hold.6 = (bf16[3072,1536]{1,0:T(8,128)(2,1)S(1)}, f32[8,128]{1,0:T(8,128)S(1)}) custom-call(f32[8,128]{1,0:T(8,128)S(1)} %get-tuple-element.67.refs_0_, bf16[3072,1536]{1,0:T(8,128)(2,1)} %refs_1_.6), custom_call_target="tpu_custom_call" | custom-call | bytes 9437184 | tf_op jit(solution)/shard_map/hold/pallas_call | solution.py:62
  43.9 1.6 %collective-permute-done.13.refs_3_ = f32[88,384]{1,0:T(8,128)S(1)} collective-permute-done((f32[88,384]{1,0:T(8,128)S(1)}, f32[88,384]{1,0:T(8,128)S(1)}, u32[]{:S(2)}, u32[]{:S(2)}) %collective-permute-start.13) | collective-permute-done | bytes 135200 | tf_op jit(solution)/shard_map/ppermute | solution.py:38
  48.3 1.6 %collective-permute-start.15 = (bf16[16,3072]{1,0:T(8,128)(2,1)S(1)}, bf16[16,3072]{1,0:T(8,128)(2,1)S(1)}, u32[]{:S(2)}, u32[]{:S(2)}) collective-permute-start(bf16[16,3072]{1,0:T(8,128)(2,1)S(1)} %get-tuple-element.82), channel_id=1, source_target_pairs={{0,1},{1,0},{2,3},{3,2},{4,5},{5,4},{6,7},{7,6},{8,9},{9,8},{10,11... | collective-permute-start | bytes 294920 | tf_op jit(solution)/shard_map/ppermute | solution.py:38
  49.9 2.1 %collective-permute-start.16 = (bf16[16,3072]{1,0:T(8,128)(2,1)S(1)}, bf16[16,3072]{1,0:T(8,128)(2,1)S(1)}, u32[]{:S(2)}, u32[]{:S(2)}) collective-permute-start(bf16[16,3072]{1,0:T(8,128)(2,1)S(1)} %get-tuple-element.83), channel_id=1, source_target_pairs={{0,2},{1,3},{2,0},{3,1},{4,6},{5,7},{6,4},{7,5},{8,10},{9,11},{10,... | collective-permute-start | bytes 294920 | tf_op jit(solution)/shard_map/ppermute | solution.py:38
  52.7 3.7 %hold.7 = (bf16[1536,3072]{1,0:T(8,128)(2,1)S(1)}, bf16[64,3072]{1,0:T(8,128)(2,1)S(1)}, f32[8,128]{1,0:T(8,128)S(1)}) custom-call(f32[8,128]{1,0:T(8,128)S(1)} %get-tuple-element.76.refs_0_, bf16[1536,3072]{1,0:T(8,128)(2,1)} %refs_1_.7, bf16[64,3072]{1,0:T(8,128)(2,1)} %refs_2_.1), custom_call_target="tpu_custom_call" | custom-call | bytes 9830400 | tf_op jit(solution)/shard_map/hold/pallas_call | solution.py:62
  56.5 4.2 %collective-permute-done.16.refs_2_ = bf16[16,3072]{1,0:T(8,128)(2,1)S(1)} collective-permute-done((bf16[16,3072]{1,0:T(8,128)(2,1)S(1)}, bf16[16,3072]{1,0:T(8,128)(2,1)S(1)}, u32[]{:S(2)}, u32[]{:S(2)}) %collective-permute-start.16) | collective-permute-done | bytes 98336 | tf_op jit(solution)/shard_map/ppermute | solution.py:38
  63.0 1.5 %collective-permute-start.18 = (bf16[16,3072]{1,0:T(8,128)(2,1)S(1)}, bf16[16,3072]{1,0:T(8,128)(2,1)S(1)}, u32[]{:S(2)}, u32[]{:S(2)}) collective-permute-start(bf16[16,3072]{1,0:T(8,128)(2,1)S(1)} %get-tuple-element.86.refs_0_), channel_id=1, source_target_pairs={{0,8},{4,12},{8,0},{12,4},{16,24},{20,28},{24,16},{28,20},{1,9},{5... | collective-permute-start | bytes 294920 | tf_op jit(solution)/shard_map/ppermute | solution.py:38
  64.5 2.1 %collective-permute-done.20.refs_3_ = bf16[16,3072]{1,0:T(8,128)(2,1)S(1)} collective-permute-done((bf16[16,3072]{1,0:T(8,128)(2,1)S(1)}, bf16[16,3072]{1,0:T(8,128)(2,1)S(1)}, u32[]{:S(2)}, u32[]{:S(2)}) %collective-permute-start.20) | collective-permute-done | bytes 98336 | tf_op jit(solution)/shard_map/ppermute | solution.py:38
  67.7 1.7 %collective-permute-done.21.refs_1_ = bf16[4,16,3072]{2,1,0:T(8,128)(2,1)S(1)} collective-permute-done((bf16[4,16,3072]{2,1,0:T(8,128)(2,1)S(1)}, bf16[4,16,3072]{2,1,0:T(8,128)(2,1)S(1)}, u32[]{:S(2)}, u32[]{:S(2)}) %collective-permute-start.21) | collective-permute-done | bytes 393248 | tf_op jit(solution)/shard_map/ppermute | solution.py:38
  69.4 2.7 %mlp.1 = (f32[64,3072]{1,0:T(8,128)S(1)}, bf16[64,3072]{1,0:T(8,128)(2,1)S(1)}) custom-call(bf16[4,16,3072]{2,1,0:T(8,128)(2,1)S(1)} %join.3.refs_0_, bf16[4,16,3072]{2,1,0:T(8,128)(2,1)S(1)} %collective-permute-done.21.refs_1_, bf16[3072,1536]{1,0:T(8,128)(2,1)S(1)} %get-tuple-element.87.refs_2_, bf16[1536,3072]{1,0:T(8,128)(2,1)S(1)} %get-tuple-element.88.refs_3_), custom_call_target="tpu_custom_call" | custom-call | tf_op jit(solution)/shard_map/mlp/pallas_call | solution.py:407
  72.3 1.6 %collective-permute-done.22.refs_1_ = bf16[64,3072]{1,0:T(8,128)(2,1)S(1)} collective-permute-done((bf16[64,3072]{1,0:T(8,128)(2,1)S(1)}, bf16[64,3072]{1,0:T(8,128)(2,1)S(1)}, u32[]{:S(2)}, u32[]{:S(2)}) %collective-permute-start.22) | collective-permute-done | bytes 393248 | tf_op jit(solution)/shard_map/ppermute | solution.py:38
  74.0 1.6 %collective-permute-start.23 = (bf16[16,3072]{1,0:T(8,128)(2,1)S(1)}, bf16[16,3072]{1,0:T(8,128)(2,1)S(1)}, u32[]{:S(2)}, u32[]{:S(2)}) collective-permute-start(bf16[16,3072]{1,0:T(8,128)(2,1)S(1)} %get-tuple-element.92), channel_id=1, source_target_pairs={{0,8},{4,12},{8,0},{12,4},{16,24},{20,28},{24,16},{28,20},{1,9},{5... | collective-permute-start | bytes 294920 | tf_op jit(solution)/shard_map/ppermute | solution.py:38
  78.9 3.4 %collective-permute-done.24.refs_2_ = bf16[16,3072]{1,0:T(8,128)(2,1)S(1)} collective-permute-done((bf16[16,3072]{1,0:T(8,128)(2,1)S(1)}, bf16[16,3072]{1,0:T(8,128)(2,1)S(1)}, u32[]{:S(2)}, u32[]{:S(2)}) %collective-permute-start.24) | collective-permute-done | bytes 98336 | tf_op jit(solution)/shard_map/ppermute | solution.py:38
  (47 shorter events, 24.0 us)
Async XLA Ops:
  2.0 10.7 %collective-permute-start = (bf16[4,64,768]{2,1,0:T(8,128)(2,1)S(1)}, bf16[4,64,768]{2,1,0:T(8,128)(2,1)S(1)}, u32[]{:S(2)}, u32[]{:S(2)}) collective-permute-start(bf16[4,64,768]{2,1,0:T(8,128)(2,1)S(1)} %get-tuple-element.52), channel_id=1, source_target_pairs={{0,4},{4,0},{8,12},{12,8},{16,20},{20,16},{24,28},{28,24},{1,5},{5... | collective-permute-start | bytes 1179656 | tf_op jit(solution)/shard_map/ppermute | solution.py:38
  2.6 9.4 %collective-permute-start.1 = (bf16[16,3200]{1,0:T(8,128)(2,1)S(1)}, bf16[16,3200]{1,0:T(8,128)(2,1)S(1)}, u32[]{:S(2)}, u32[]{:S(2)}) collective-permute-start(bf16[16,3200]{1,0:T(8,128)(2,1)S(1)} %get-tuple-element.53.refs_0_), channel_id=1, source_target_pairs={{0,2},{1,3},{2,0},{3,1},{4,6},{5,7},{6,4},{7,5},{8,10},{9,11},{10,... | collective-permute-start | bytes 307208 | tf_op jit(solution)/shard_map/ppermute | solution.py:38
  6.2 10.0 %collective-permute-start.2 = (bf16[16,3200]{1,0:T(8,128)(2,1)S(1)}, bf16[16,3200]{1,0:T(8,128)(2,1)S(1)}, u32[]{:S(2)}, u32[]{:S(2)}) collective-permute-start(bf16[16,3200]{1,0:T(8,128)(2,1)S(1)} %get-tuple-element.53.refs_0_), channel_id=1, source_target_pairs={{0,1},{1,0},{2,3},{3,2},{4,5},{5,4},{6,7},{7,6},{8,9},{9,8},{10,11... | collective-permute-start | bytes 307208 | tf_op jit(solution)/shard_map/ppermute | solution.py:38
  12.0 4.7 %collective-permute-start.3 = (bf16[16,3200]{1,0:T(8,128)(2,1)S(1)}, bf16[16,3200]{1,0:T(8,128)(2,1)S(1)}, u32[]{:S(2)}, u32[]{:S(2)}) collective-permute-start(bf16[16,3200]{1,0:T(8,128)(2,1)S(1)} %relay.1.refs_2_.refs_4_), channel_id=1, source_target_pairs={{0,1},{1,0},{2,3},{3,2},{4,5},{5,4},{6,7},{7,6},{8,9},{9,8},{10,11... | collective-permute-start | bytes 307208 | tf_op jit(solution)/shard_map/ppermute | solution.py:38
  12.7 20.5 %collective-permute-start.8 = (bf16[2,64,768]{2,1,0:T(8,128)(2,1)S(1)}, bf16[2,64,768]{2,1,0:T(8,128)(2,1)S(1)}, u32[]{:S(2)}, u32[]{:S(2)}) collective-permute-start(bf16[2,64,768]{2,1,0:T(8,128)(2,1)S(1)} %get-tuple-element.63), channel_id=1, source_target_pairs={{0,2},{1,3},{2,0},{3,1},{4,6},{5,7},{6,4},{7,5},{8,10},{9,11},{10,... | collective-permute-start | bytes 589832 | tf_op jit(solution)/shard_map/ppermute | solution.py:38
  18.8 14.5 %collective-permute-start.10 = (bf16[2,64,768]{2,1,0:T(8,128)(2,1)S(1)}, bf16[2,64,768]{2,1,0:T(8,128)(2,1)S(1)}, u32[]{:S(2)}, u32[]{:S(2)}) collective-permute-start(bf16[2,64,768]{2,1,0:T(8,128)(2,1)S(1)} %get-tuple-element.66), channel_id=1, source_target_pairs={{0,1},{1,0},{2,3},{3,2},{4,5},{5,4},{6,7},{7,6},{8,9},{9,8},{10,11... | collective-permute-start | bytes 589832 | tf_op jit(solution)/shard_map/ppermute | solution.py:38
  19.6 13.7 %collective-permute-start.9 = (bf16[2,64,768]{2,1,0:T(8,128)(2,1)S(1)}, bf16[2,64,768]{2,1,0:T(8,128)(2,1)S(1)}, u32[]{:S(2)}, u32[]{:S(2)}) collective-permute-start(bf16[2,64,768]{2,1,0:T(8,128)(2,1)S(1)} %get-tuple-element.64), channel_id=1, source_target_pairs={{0,3},{1,2},{2,1},{3,0},{4,7},{5,6},{6,5},{7,4},{8,11},{9,10},{10,... | collective-permute-start | bytes 589832 | tf_op jit(solution)/shard_map/ppermute | solution.py:38
  24.8 4.2 %collective-permute-start.6 = (bf16[2,40,384]{2,1,0:T(8,128)(2,1)S(1)}, bf16[2,40,384]{2,1,0:T(8,128)(2,1)S(1)}, u32[]{:S(2)}, u32[]{:S(2)}) collective-permute-start(bf16[2,40,384]{2,1,0:T(8,128)(2,1)S(1)} %join.2.refs_0_), channel_id=1, source_target_pairs={{0,16},{4,20},{8,24},{12,28},{16,0},{20,4},{24,8},{28,12},{1,17},{... | collective-permute-start | bytes 184328 | tf_op jit(solution)/shard_map/ppermute | solution.py:38
  26.4 6.6 %collective-permute-start.5 = (bf16[2,40,384]{2,1,0:T(8,128)(2,1)S(1)}, bf16[2,40,384]{2,1,0:T(8,128)(2,1)S(1)}, u32[]{:S(2)}, u32[]{:S(2)}) collective-permute-start(bf16[2,40,384]{2,1,0:T(8,128)(2,1)S(1)} %join.2.refs_0_), channel_id=1, source_target_pairs={{0,8},{4,12},{8,0},{12,4},{16,24},{20,28},{24,16},{28,20},{1,9},{5... | collective-permute-start | bytes 184328 | tf_op jit(solution)/shard_map/ppermute | solution.py:38
  29.1 4.2 %collective-permute-start.7 = (bf16[2,40,384]{2,1,0:T(8,128)(2,1)S(1)}, bf16[2,40,384]{2,1,0:T(8,128)(2,1)S(1)}, u32[]{:S(2)}, u32[]{:S(2)}) collective-permute-start(bf16[2,40,384]{2,1,0:T(8,128)(2,1)S(1)} %collective-permute-done.6.refs_2_), channel_id=1, source_target_pairs={{0,8},{4,12},{8,0},{12,4},{16,24},{20,28},{24,16},{28,20},{1,9},{5... | collective-permute-start | bytes 184328 | tf_op jit(solution)/shard_map/ppermute | solution.py:38
  36.5 7.2 %collective-permute-start.11 = (f32[88,384]{1,0:T(8,128)S(1)}, f32[88,384]{1,0:T(8,128)S(1)}, u32[]{:S(2)}, u32[]{:S(2)}) collective-permute-start(f32[88,384]{1,0:T(8,128)S(1)} %get-tuple-element.70), channel_id=1, source_target_pairs={{0,8},{4,12},{8,0},{12,4},{16,24},{20,28},{24,16},{28,20},{1,9},{5... | collective-permute-start | bytes 405512 | tf_op jit(solution)/shard_map/ppermute | solution.py:38
  38.1 5.8 %collective-permute-start.12 = (f32[88,384]{1,0:T(8,128)S(1)}, f32[88,384]{1,0:T(8,128)S(1)}, u32[]{:S(2)}, u32[]{:S(2)}) collective-permute-start(f32[88,384]{1,0:T(8,128)S(1)} %get-tuple-element.71), channel_id=1, source_target_pairs={{0,16},{4,20},{8,24},{12,28},{16,0},{20,4},{24,8},{28,12},{1,17},{... | collective-permute-start | bytes 405512 | tf_op jit(solution)/shard_map/ppermute | solution.py:38
  39.6 5.9 %collective-permute-start.13 = (f32[88,384]{1,0:T(8,128)S(1)}, f32[88,384]{1,0:T(8,128)S(1)}, u32[]{:S(2)}, u32[]{:S(2)}) collective-permute-start(f32[88,384]{1,0:T(8,128)S(1)} %get-tuple-element.72), channel_id=1, source_target_pairs={{0,24},{4,28},{8,16},{12,20},{16,8},{20,12},{24,0},{28,4},{1,25},{... | collective-permute-start | bytes 405512 | tf_op jit(solution)/shard_map/ppermute | solution.py:38
  48.3 8.2 %collective-permute-start.15 = (bf16[16,3072]{1,0:T(8,128)(2,1)S(1)}, bf16[16,3072]{1,0:T(8,128)(2,1)S(1)}, u32[]{:S(2)}, u32[]{:S(2)}) collective-permute-start(bf16[16,3072]{1,0:T(8,128)(2,1)S(1)} %get-tuple-element.82), channel_id=1, source_target_pairs={{0,1},{1,0},{2,3},{3,2},{4,5},{5,4},{6,7},{7,6},{8,9},{9,8},{10,11... | collective-permute-start | bytes 294920 | tf_op jit(solution)/shard_map/ppermute | solution.py:38
  49.9 10.7 %collective-permute-start.16 = (bf16[16,3072]{1,0:T(8,128)(2,1)S(1)}, bf16[16,3072]{1,0:T(8,128)(2,1)S(1)}, u32[]{:S(2)}, u32[]{:S(2)}) collective-permute-start(bf16[16,3072]{1,0:T(8,128)(2,1)S(1)} %get-tuple-element.83), channel_id=1, source_target_pairs={{0,2},{1,3},{2,0},{3,1},{4,6},{5,7},{6,4},{7,5},{8,10},{9,11},{10,... | collective-permute-start | bytes 294920 | tf_op jit(solution)/shard_map/ppermute | solution.py:38
  52.0 8.6 %collective-permute-start.17 = (bf16[16,3072]{1,0:T(8,128)(2,1)S(1)}, bf16[16,3072]{1,0:T(8,128)(2,1)S(1)}, u32[]{:S(2)}, u32[]{:S(2)}) collective-permute-start(bf16[16,3072]{1,0:T(8,128)(2,1)S(1)} %get-tuple-element.84), channel_id=1, source_target_pairs={{0,3},{1,2},{2,1},{3,0},{4,7},{5,6},{6,5},{7,4},{8,11},{9,10},{10,... | collective-permute-start | bytes 294920 | tf_op jit(solution)/shard_map/ppermute | solution.py:38
  61.0 5.7 %collective-permute-start.20 = (bf16[16,3072]{1,0:T(8,128)(2,1)S(1)}, bf16[16,3072]{1,0:T(8,128)(2,1)S(1)}, u32[]{:S(2)}, u32[]{:S(2)}) collective-permute-start(bf16[16,3072]{1,0:T(8,128)(2,1)S(1)} %get-tuple-element.86.refs_0_), channel_id=1, source_target_pairs={{0,24},{4,28},{8,16},{12,20},{16,8},{20,12},{24,0},{28,4},{1,25},{... | collective-permute-start | bytes 294920 | tf_op jit(solution)/shard_map/ppermute | solution.py:38
  61.8 5.7 %collective-permute-start.19 = (bf16[16,3072]{1,0:T(8,128)(2,1)S(1)}, bf16[16,3072]{1,0:T(8,128)(2,1)S(1)}, u32[]{:S(2)}, u32[]{:S(2)}) collective-permute-start(bf16[16,3072]{1,0:T(8,128)(2,1)S(1)} %get-tuple-element.86.refs_0_), channel_id=1, source_target_pairs={{0,16},{4,20},{8,24},{12,28},{16,0},{20,4},{24,8},{28,12},{1,17},{... | collective-permute-start | bytes 294920 | tf_op jit(solution)/shard_map/ppermute | solution.py:38
  63.0 4.6 %collective-permute-start.18 = (bf16[16,3072]{1,0:T(8,128)(2,1)S(1)}, bf16[16,3072]{1,0:T(8,128)(2,1)S(1)}, u32[]{:S(2)}, u32[]{:S(2)}) collective-permute-start(bf16[16,3072]{1,0:T(8,128)(2,1)S(1)} %get-tuple-element.86.refs_0_), channel_id=1, source_target_pairs={{0,8},{4,12},{8,0},{12,4},{16,24},{20,28},{24,16},{28,20},{1,9},{5... | collective-permute-start | bytes 294920 | tf_op jit(solution)/shard_map/ppermute | solution.py:38
  67.6 1.8 %collective-permute-start.21 = (bf16[4,16,3072]{2,1,0:T(8,128)(2,1)S(1)}, bf16[4,16,3072]{2,1,0:T(8,128)(2,1)S(1)}, u32[]{:S(2)}, u32[]{:S(2)}) collective-permute-start(bf16[4,16,3072]{2,1,0:T(8,128)(2,1)S(1)} %join.3.refs_0_), channel_id=1, source_target_pairs={{0,4},{4,0},{8,12},{12,8},{16,20},{20,16},{24,28},{28,24},{1,5},{5... | collective-permute-start | bytes 1179656 | tf_op jit(solution)/shard_map/ppermute | solution.py:38
  72.1 1.8 %collective-permute-start.22 = (bf16[64,3072]{1,0:T(8,128)(2,1)S(1)}, bf16[64,3072]{1,0:T(8,128)(2,1)S(1)}, u32[]{:S(2)}, u32[]{:S(2)}) collective-permute-start(bf16[64,3072]{1,0:T(8,128)(2,1)S(1)} %get-tuple-element.90), channel_id=1, source_target_pairs={{0,4},{4,0},{8,12},{12,8},{16,20},{20,16},{24,28},{28,24},{1,5},{5... | collective-permute-start | bytes 1179656 | tf_op jit(solution)/shard_map/ppermute | solution.py:38
  74.0 4.9 %collective-permute-start.23 = (bf16[16,3072]{1,0:T(8,128)(2,1)S(1)}, bf16[16,3072]{1,0:T(8,128)(2,1)S(1)}, u32[]{:S(2)}, u32[]{:S(2)}) collective-permute-start(bf16[16,3072]{1,0:T(8,128)(2,1)S(1)} %get-tuple-element.92), channel_id=1, source_target_pairs={{0,8},{4,12},{8,0},{12,4},{16,24},{20,28},{24,16},{28,20},{1,9},{5... | collective-permute-start | bytes 294920 | tf_op jit(solution)/shard_map/ppermute | solution.py:38
  75.6 6.7 %collective-permute-start.24 = (bf16[16,3072]{1,0:T(8,128)(2,1)S(1)}, bf16[16,3072]{1,0:T(8,128)(2,1)S(1)}, u32[]{:S(2)}, u32[]{:S(2)}) collective-permute-start(bf16[16,3072]{1,0:T(8,128)(2,1)S(1)} %get-tuple-element.93), channel_id=1, source_target_pairs={{0,16},{4,20},{8,24},{12,28},{16,0},{20,4},{24,8},{28,12},{1,17},{... | collective-permute-start | bytes 294920 | tf_op jit(solution)/shard_map/ppermute | solution.py:38
  76.5 5.8 %collective-permute-start.25 = (bf16[16,3072]{1,0:T(8,128)(2,1)S(1)}, bf16[16,3072]{1,0:T(8,128)(2,1)S(1)}, u32[]{:S(2)}, u32[]{:S(2)}) collective-permute-start(bf16[16,3072]{1,0:T(8,128)(2,1)S(1)} %get-tuple-element.94), channel_id=1, source_target_pairs={{0,24},{4,28},{8,16},{12,20},{16,8},{20,12},{24,0},{28,4},{1,25},{... | collective-permute-start | bytes 294920 | tf_op jit(solution)/shard_map/ppermute | solution.py:38
  (2 other events, 2.5 us)
where the time goes:
time: 83.6 us; the launch traced here: 83.3 us
  starting transfers between devices  34.7 us (42%)
  Pallas kernels  25 us (30%)
  waiting for transfers between devices  23.5 us (28%)
    ppermute x26, starting transfers between devices, trade(): lax.ppermute(x, axis, [(i, i ^ flip) for i in range(lax.axis_size(axis))])  34.7 us
    ppermute x26, waiting for transfers between devices, trade(): lax.ppermute(x, axis, [(i, i ^ flip) for i in range(lax.axis_size(axis))])  23.5 us
    pallas_call x4, Pallas kernels, hold(): pl.pallas_call(functools.partial(hold_kernel, count), in_specs=[VMEM_SPEC...  12.1 us
    pallas_call x1, Pallas kernels, attend(): pl.pallas_call(functools.partial(attend_kernel, len(queries)), out_shape=...  3.24 us
    pallas_call x1, Pallas kernels, mlp(): pl.pallas_call(functools.partial(mlp_kernel, len(rows)), out_shape=[jax.S...  2.7 us
    pallas_call x1, Pallas kernels, enter(): pl.pallas_call(functools.partial(enter_kernel, pair), in_specs=[ANY_SPEC]...  2.02 us
  transfers between devices with their start and end apart: 26, of which 16 were waited for; matrix products, arithmetic and copies ran while one was open for 0% of the time, Pallas kernels for 17%

commit v1 on v0

--- a/solution.py
+++ b/solution.py
@@ -23,6 +23,37 @@
         if k in on_arrival:
             have[k] = on_arrival[k](have[k])
     return [have[k] for k in range(count)]
+
+
+def pack_shared(shared, share):
+    step = shared.shape[1] // 8
+    per = 8 // share
+    row = lax.broadcasted_iota(jnp.int32, (8, step), 0)
+    blocks = []
+    for first in range(0, 8, per):
+        block = shared[:, first * step : (first + 1) * step]
+        for i in range(1, per):
+            piece = shared[:, (first + i) * step : (first + i + 1) * step]
+            block = jnp.where(row >= i * share, pltpu.roll(piece, i * share, axis=0), block)
+        blocks.append(block)
+    return jnp.concatenate(blocks, axis=0)
+
+
+def pack(main, shared, share):
+    step = main.shape[1] // 8
+    blocks = [main[:, c * step : (c + 1) * step] for c in range(8)]
+    return jnp.concatenate(blocks + [pack_shared(shared, share)], axis=0)
+
+
+def unpack(packed, share):
+    per = 8 // share
+    main, shared = [], []
+    for c in range(8):
+        main.append(packed[8 * c : 8 * c + 8])
+        block = packed[64 + 8 * (c // per) : 72 + 8 * (c // per)]
+        shift = (8 - share * (c % per)) % 8
+        shared.append(pltpu.roll(block, shift, axis=0) if shift else block)
+    return jnp.concatenate(main, axis=1), jnp.concatenate(shared, axis=1)
 
 
 def layer_norm(row_block, shift_by, scale_by):
@@ -342,12 +373,18 @@
     )(after, *parts)
 
 
-def output_kernel(sides, spread_ref, *refs):
-    side_refs, w_ref, (*out_refs, token_ref) = refs[:sides], refs[sides], refs[sides + 1 :]
+def output_kernel(sides, share, spread_ref, rows_ref, mod_ref, *refs):
+    side_refs, w_ref = refs[:sides], refs[sides]
+    own_ref, *out_refs, token_ref, terms_ref = refs[sides + 1 :]
     token_ref[...] = jnp.zeros_like(token_ref)
     group, half = side_refs[0].shape
-    slots, width = out_refs[0].shape
-    spread = spread_ref[:, :group]
+    slots, width = rows_ref.shape
+    spread = spread_ref[...].astype(jnp.float32)
+    parts = spread.shape[0] // slots
+    main = [spread[k * slots : k * slots + 8] for k in range(parts)]
+    shared = [spread[k * slots + 8 : k * slots + 16] for k in range(parts)]
+    spread = jnp.concatenate(main + [sum(shared[1:], shared[0])], axis=0)
+    spread = spread.astype(jnp.bfloat16)[:, :group]
     attended = [
         jnp.dot(spread, ref[...], preferred_element_type=jnp.float32).astype(jnp.bfloat16)
         for ref in side_refs
@@ -361,56 +398,71 @@
             terms = terms + jnp.dot(
                 side, w_ref[pl.ds(start, half), col : col + step], preferred_element_type=jnp.float32
             )
-        for k, out_ref in enumerate(out_refs):
-            piece = terms[k * slots : (k + 1) * slots]
-            out_ref[:, col : col + step] = piece.astype(out_ref.dtype)
-
-
-def output(spread, sides, w_out, slots, parts):
-    width = w_out.shape[1]
-    return pl.pallas_call(
-        functools.partial(output_kernel, len(sides)),
-        out_shape=[
-            jax.ShapeDtypeStruct((slots, width), jnp.bfloat16 if k else jnp.float32)
-            for k in range(parts)
-        ]
-        + [TOKEN],
+        terms_ref[:, col : col + step] = terms
+    uly = lax.axis_index("uly")
+    shared = mod_ref[2:3, :] * terms_ref[8 * parts :, :] + rows_ref[8:, :]
+    for k in range(parts):
+        main = terms_ref[8 * k : 8 * k + 8, :]
+        rows = pltpu.roll(shared, lax.rem(8 - share * (uly ^ k), 8), axis=0)
+        if k == 0:
+            own_ref[:8, :] = main
+            own_ref[8:, :] = rows
+        else:
+            out_refs[k - 1][...] = pack(main, rows, share).astype(jnp.bfloat16)
+
+
+def output(spread, rows_in, modulation, sides, w_out, parts, share):
+    slots, width = rows_in.shape
+    packed = jax.ShapeDtypeStruct((64 + 8 * share, width // 8), jnp.bfloat16)
+    own = jax.ShapeDtypeStruct((slots, width), jnp.float32)
+    return pl.pallas_call(
+        functools.partial(output_kernel, len(sides), share),
+        out_shape=[own] + [packed] * (parts - 1) + [TOKEN],
+        scratch_shapes=[pltpu.VMEM((8 * parts + 8, width), jnp.float32)],
         compiler_params=pltpu.CompilerParams(vmem_limit_bytes=16 << 20),
         name="output",
-    )(spread, *sides, w_out)
-
-
-def mlp_kernel(pieces, *refs):
+    )(spread, rows_in, modulation, *sides, w_out)
+
+
+def mlp_kernel(pieces, share, *refs):
     row_refs, (up_ref, down_ref) = refs[:pieces], refs[pieces : pieces + 2]
-    *out_refs, act_ref = refs[pieces + 2 :]
+    *out_refs, act_ref, terms_ref = refs[pieces + 2 :]
     hidden, width = down_ref.shape
-    rows = [ref[j] for ref in row_refs for j in range(ref.shape[0])]
-    rows = jnp.concatenate(rows, axis=0)
-    count = out_refs[0].shape[0]
+    rows = []
+    for ref in row_refs:
+        for j in range(ref.shape[0]):
+            rows += unpack(ref[j].astype(jnp.float32), share)
+    rows = jnp.concatenate(rows, axis=0).astype(jnp.bfloat16)
     step = math.gcd(hidden, 512)
     for col in range(0, hidden, step):
         lifted = jnp.dot(rows, up_ref[:, col : col + step], preferred_element_type=jnp.float32)
         act_ref[:, col : col + step] = jax.nn.gelu(lifted, approximate=True).astype(jnp.bfloat16)
     step = math.gcd(width, 512)
     for col in range(0, width, step):
-        down = jnp.dot(
+        terms_ref[:, col : col + step] = jnp.dot(
             act_ref[...], down_ref[:, col : col + step], preferred_element_type=jnp.float32
         )
-        for side, out_ref in enumerate(out_refs):
-            piece = down[side * count : (side + 1) * count]
-            out_ref[:, col : col + step] = piece.astype(out_ref.dtype)
-
-
-def mlp(rows, w_up, w_down, pair):
-    count = sum(x.shape[0] * x.shape[1] for x in rows)
+    for side, out_ref in enumerate(out_refs):
+        count = out_ref.shape[0]
+        for j in range(count):
+            at = 16 * (side * count + j)
+            packed = pack(terms_ref[at : at + 8, :], terms_ref[at + 8 : at + 16, :], share)
+            out_ref[j] = packed.astype(out_ref.dtype)
+
+
+def mlp(rows, w_up, w_down, share):
     hidden, width = w_down.shape
-    return pl.pallas_call(
-        functools.partial(mlp_kernel, len(rows)),
+    count = 16 * sum(x.shape[0] for x in rows)
+    return pl.pallas_call(
+        functools.partial(mlp_kernel, len(rows), share),
         out_shape=[
-            jax.ShapeDtypeStruct((count // pair, width), jnp.bfloat16 if side else jnp.float32)
-            for side in range(pair)
+            jax.ShapeDtypeStruct(x.shape, jnp.bfloat16 if side else jnp.float32)
+            for side, x in enumerate(rows)
         ],
-        scratch_shapes=[pltpu.VMEM((count, hidden), jnp.bfloat16)],
+        scratch_shapes=[
+            pltpu.VMEM((count, hidden), jnp.bfloat16),
+            pltpu.VMEM((count, width), jnp.float32),
+        ],
         compiler_params=pltpu.CompilerParams(vmem_limit_bytes=32 << 20),
         name="mlp",
     )(*rows, w_up, w_down)
@@ -431,22 +483,29 @@
     )(*parts, *after)
 
 
-def renorm_kernel(hold_ref, rows_ref, mod_ref, *refs):
+def total_of(refs):
+    total = refs[0][...].astype(jnp.float32)
+    for ref in refs[1:]:
+        total = total + ref[...].astype(jnp.float32)
+    return total
+
+
+def renorm_kernel(share, hold_ref, rows_ref, mod_ref, own_ref, *refs):
     *term_refs, after_ref, normed_ref = refs
-    branch = term_refs[0][...]
-    for ref in term_refs[1:]:
-        branch = branch + ref[...].astype(jnp.float32)
-    after = rows_ref[...] + mod_ref[2:3, :] * branch
+    main, shared = unpack(total_of(term_refs), share)
+    main = rows_ref[:8, :] + mod_ref[2:3, :] * (own_ref[:8, :] + main)
+    after = jnp.concatenate([main, own_ref[8:, :] + shared], axis=0)
     after_ref[...] = after
-    normed_ref[...] = layer_norm(after, mod_ref[3:4, :], mod_ref[4:5, :]).astype(jnp.bfloat16)
-
-
-def renorm(after, rows_in, modulation, terms):
-    return pl.pallas_call(
-        renorm_kernel,
+    normed = layer_norm(after, mod_ref[3:4, :], mod_ref[4:5, :])
+    normed_ref[...] = pack(normed[:8], normed[8:], share).astype(jnp.bfloat16)
+
+
+def renorm(after, rows_in, modulation, terms, share):
+    return pl.pallas_call(
+        functools.partial(renorm_kernel, share),
         out_shape=[
             jax.ShapeDtypeStruct(rows_in.shape, jnp.float32),
-            jax.ShapeDtypeStruct(rows_in.shape, jnp.bfloat16),
+            jax.ShapeDtypeStruct(terms[1].shape, jnp.bfloat16),
         ],
         compiler_params=pltpu.CompilerParams(vmem_limit_bytes=8 << 20),
         name="renorm",
@@ -455,47 +514,94 @@
 
 def fold_kernel(sides, *refs):
     side_refs, out_refs = refs[:sides], refs[sides:]
-    slots = out_refs[0].shape[0]
     for j, out_ref in enumerate(out_refs):
-        total = side_refs[0][j * slots : (j + 1) * slots]
-        for ref in side_refs[1:]:
-            total = total + ref[j * slots : (j + 1) * slots].astype(jnp.float32)
-        out_ref[...] = total.astype(out_ref.dtype)
-
-
-def fold(sides, slots):
-    count, width = sides[0].shape
+        out_ref[...] = total_of([ref.at[j] for ref in side_refs]).astype(out_ref.dtype)
+
+
+def fold(sides):
+    chips, *shape = sides[0].shape
     return pl.pallas_call(
         functools.partial(fold_kernel, len(sides)),
         out_shape=[
-            jax.ShapeDtypeStruct((slots, width), jnp.bfloat16 if j else jnp.float32)
-            for j in range(count // slots)
+            jax.ShapeDtypeStruct(shape, jnp.bfloat16 if j else jnp.float32) for j in range(chips)
         ],
         compiler_params=pltpu.CompilerParams(vmem_limit_bytes=8 << 20),
         name="fold",
     )(*sides)
 
 
-def finish_kernel(select_ref, cached_ref, after_ref, mod_ref, *refs):
-    *term_refs, out_ref = refs
-    total = term_refs[0][...]
-    for ref in term_refs[1:]:
-        total = total + ref[...].astype(jnp.float32)
-    renewed = (after_ref[...] + mod_ref[5:6, :] * total).astype(jnp.bfloat16)
+def renew_kernel(share, after_ref, mod_ref, *refs):
+    *term_refs, main_ref, shared_ref = refs
+    main, shared = unpack(total_of(term_refs), share)
+    gate = mod_ref[5:6, :]
+    main_ref[...] = after_ref[:8, :] + gate * main
+    shared = pack_shared(after_ref[8:, :] + gate * shared, share)
+    shared_ref[...] = shared.astype(jnp.bfloat16)
+
+
+def renew(after_attn, modulation, terms, share):
+    width = after_attn.shape[1]
+    return pl.pallas_call(
+        functools.partial(renew_kernel, share),
+        out_shape=[
+            jax.ShapeDtypeStruct((8, width), jnp.float32),
+            jax.ShapeDtypeStruct((8 * share, width // 8), jnp.bfloat16),
+        ],
+        compiler_params=pltpu.CompilerParams(vmem_limit_bytes=8 << 20),
+        name="renew",
+    )(after_attn, modulation, *terms)
+
+
+def place_kernel(select_ref, cached_ref, main_ref, out_ref):
     select = select_ref[...]
-    placed = jnp.dot(select, renewed, preferred_element_type=jnp.float32)
+    main = main_ref[...]
+    rows = jnp.concatenate([main, jnp.zeros_like(main)], axis=0).astype(jnp.bfloat16)
+    placed = jnp.dot(select, rows, preferred_element_type=jnp.float32)
     covered = jnp.sum(select.astype(jnp.float32), axis=1, keepdims=True)
-    blended = cached_ref[...].astype(jnp.float32) * (1.0 - covered) + placed
-    out_ref[...] = blended.astype(jnp.bfloat16)
-
-
-def finish(select, cached, after_attn, modulation, terms):
-    return pl.pallas_call(
-        finish_kernel,
-        out_shape=jax.ShapeDtypeStruct(cached.shape, jnp.bfloat16),
+    out_ref[...] = cached_ref[...].astype(jnp.float32) * (1.0 - covered) + placed
+
+
+def place(select, cached, main):
+    return pl.pallas_call(
+        place_kernel,
+        out_shape=jax.ShapeDtypeStruct(cached.shape, jnp.float32),
+        compiler_params=pltpu.CompilerParams(vmem_limit_bytes=8 << 20),
+        name="place",
+    )(select, cached, main)
+
+
+def finish_kernel(share, select_ref, placed_ref, *refs):
+    *shared_refs, out_ref, stack_ref = refs
+    parts, _, step = stack_ref.shape
+    for k, ref in enumerate(shared_refs):
+        stack_ref[k] = ref[...].astype(jnp.float32)
+    uly = lax.axis_index("uly")
+    per = 8 // share
+    row = lax.broadcasted_iota(jnp.int32, (8, step), 0)
+    blocks = [jnp.zeros((8, step), jnp.float32) for _ in range(8)]
+    for part in range(parts):
+        packed = stack_ref[uly ^ part]
+        for c in range(8):
+            block = packed[8 * (c // per) : 8 * (c // per) + 8]
+            shift = share * (part - c % per) % 8
+            if shift:
+                block = pltpu.roll(block, shift, axis=0)
+            wanted = (row >= share * part) & (row < share * (part + 1))
+            blocks[c] = jnp.where(wanted, block, blocks[c])
+    shared = jnp.concatenate(blocks, axis=1)
+    rows = jnp.concatenate([jnp.zeros_like(shared), shared], axis=0).astype(jnp.bfloat16)
+    placed = jnp.dot(select_ref[...], rows, preferred_element_type=jnp.float32)
+    out_ref[...] = (placed_ref[...] + placed).astype(jnp.bfloat16)
+
+
+def finish(select, placed, shared, share):
+    return pl.pallas_call(
+        functools.partial(finish_kernel, share),
+        out_shape=jax.ShapeDtypeStruct(placed.shape, jnp.bfloat16),
+        scratch_shapes=[pltpu.VMEM((len(shared), *shared[0].shape), jnp.float32)],
         compiler_params=pltpu.CompilerParams(vmem_limit_bytes=8 << 20),
         name="finish",
-    )(select, cached, after_attn, modulation, *terms)
+    )(select, placed, *shared)
 
 
 def body(
@@ -518,6 +624,7 @@
     group = min(slots * uly_size, slots + (uly_size - 1) * OTHER)
     pair = 2 if blk_size % 2 == 0 and local_heads % 2 == 0 else 1
     chips = blk_size // pair
+    share = (slots - OTHER) // uly_size
 
     rows_in, normed, select, modulation, sides = enter(
         refresh_idx, hidden_in, modulation, cache_keys, cache_values, uly_size, pair
@@ -542,18 +649,20 @@
     parts = [trade(x, "blk", j * pair) for j, x in enumerate(parts)]
     attended = combine(token, parts, group, pair)
     attended = [trade(x, "blk", side) for side, x in enumerate(attended)]
-    *terms, token = output(spread, attended, w_out, slots, uly_size)
+    *terms, token = output(spread, rows_in, modulation, attended, w_out, uly_size, share)
     w_down, cached, token = hold(token, w_down, cached_out)
     terms = [trade(x, "uly", k) for k, x in enumerate(terms)]
-    after_attn, norm_mlp = renorm(token, rows_in, modulation, terms)
+    after_attn, norm_mlp = renorm(token, rows_in, modulation, terms, share)
 
     rows = [join([trade(norm_mlp, "blk", j * pair) for j in range(chips)])]
     if pair == 2:
         rows.append(trade(rows[0], "blk", 1))
-    down = mlp(rows, w_up, w_down, pair)
+    down = mlp(rows, w_up, w_down, share)
     down = [trade(x, "blk", side) for side, x in enumerate(down)]
-    terms = [trade(x, "blk", j * pair) for j, x in enumerate(fold(down, slots))]
-    return finish(select, cached, after_attn, modulation, terms)
+    terms = [trade(x, "blk", j * pair) for j, x in enumerate(fold(down))]
+    main, shared = renew(after_attn, modulation, terms, share)
+    shared = [trade(shared, "uly", k) for k in range(uly_size)]
+    return finish(select, place(select, cached, main), shared, share)
 
 
 def solution(mesh):

time: 83.6 us -> 86.4 us (1.033)
  starting transfers between devices: 34.7 us -> 39.1 us
  waiting for transfers between devices: 23.5 us -> 21.6 us
    ppermute x26 -> x29, starting transfers between devices: 34.7 us -> 39.1 us  [trade(): lax.ppermute(x, axis, [(i, i ^ flip) for i in range(lax.axis_size(axis))])]
    ppermute x26 -> x29, waiting for transfers between devices: 23.5 us -> 21.6 us  [trade(): lax.ppermute(x, axis, [(i, i ^ flip) for i in range(lax.axis_size(axis))])]
    pallas_call x4 -> x6, Pallas kernels: 5.07 us -> 5.35 us  [the longest x1 2.72 us: mlp(): pl.pallas_call(functools.partial(mlp_kernel, len(rows), share), out_shape...]
  transfers between devices with their start and end apart: 26 -> 29, of which waited for: 16 -> 20; matrix products, arithmetic and copies ran while one was open for 0% -> 0% of each run, Pallas kernels for 17% -> 17%
where the time goes in v1:
time: 86.4 us; the launch traced here: 86.2 us
  starting transfers between devices  39.1 us (45%)
  Pallas kernels  25.3 us (29%)
  waiting for transfers between devices  21.6 us (25%)
    ppermute x29, starting transfers between devices, trade(): lax.ppermute(x, axis, [(i, i ^ flip) for i in range(lax.axis_size(axis))])  39.1 us
    ppermute x29, waiting for transfers between devices, trade(): lax.ppermute(x, axis, [(i, i ^ flip) for i in range(lax.axis_size(axis))])  21.6 us
    pallas_call x4, Pallas kernels, hold(): pl.pallas_call(functools.partial(hold_kernel, count), in_specs=[VMEM_SPEC...  12.1 us
    pallas_call x1, Pallas kernels, attend(): pl.pallas_call(functools.partial(attend_kernel, len(queries)), out_shape=...  3.24 us
    pallas_call x1, Pallas kernels, mlp(): pl.pallas_call(functools.partial(mlp_kernel, len(rows), share), out_shape...  2.72 us
    pallas_call x1, Pallas kernels, enter(): pl.pallas_call(functools.partial(enter_kernel, pair), in_specs=[ANY_SPEC]...  2.02 us
  transfers between devices with their start and end apart: 29, of which 20 were waited for; matrix products, arithmetic and copies ran while one was open for 0% of the time, Pallas kernels for 17%

profile of v1, /device:TPU:0, one launch (start us, length us, event | category | flops | bytes accessed | tf_op | source)
XLA Modules:
  0.0 86.2 jit_solution(3897423951126326469)
XLA Ops:
  0.0 2.0 %enter.1 = (f32[16,3072]{1,0:T(8,128)S(1)}, bf16[16,3200]{1,0:T(8,128)(2,1)S(1)}, bf16[64,16]{1,0:T(8,128)(2,1)S(1)}, f32[6,3072]{1,0:T(8,128)S(1)}, bf16[4,64,7...) custom-call(s32[1,16]{1,0:T(1,128)} %bitcast.2, bf16[64,3072]{1,0:T(8,128)(2,1)} %hidden_hbm.1, f32[6,3072]{1,0:T(8,128)} %mod_hbm.1, ...), custom_call_target="tpu_custom_call" | custom-call | tf_op jit(solution)/shard_map/enter/pallas_call | solution.py:164
  2.6 3.7 %collective-permute-start.1 = (bf16[16,3200]{1,0:T(8,128)(2,1)S(1)}, bf16[16,3200]{1,0:T(8,128)(2,1)S(1)}, u32[]{:S(2)}, u32[]{:S(2)}) collective-permute-start(bf16[16,3200]{1,0:T(8,128)(2,1)S(1)} %get-tuple-element.55.refs_0_), channel_id=1, source_target_pairs={{0,2},{1,3},{2,0},{3,1},{4,6},{5,7},{6,4},{7,5},{8,10},{9,11},{10,... | collective-permute-start | bytes 307208 | tf_op jit(solution)/shard_map/ppermute | solution.py:69
  6.2 1.6 %collective-permute-start.2 = (bf16[16,3200]{1,0:T(8,128)(2,1)S(1)}, bf16[16,3200]{1,0:T(8,128)(2,1)S(1)}, u32[]{:S(2)}, u32[]{:S(2)}) collective-permute-start(bf16[16,3200]{1,0:T(8,128)(2,1)S(1)} %get-tuple-element.55.refs_0_), channel_id=1, source_target_pairs={{0,1},{1,0},{2,3},{3,2},{4,5},{5,4},{6,7},{7,6},{8,9},{9,8},{10,11... | collective-permute-start | bytes 307208 | tf_op jit(solution)/shard_map/ppermute | solution.py:69
  7.8 2.3 %hold.4 = (bf16[3072,768]{1,0:T(8,128)(2,1)S(1)}, f32[8,128]{1,0:T(8,128)S(1)}) custom-call(bf16[16,3200]{1,0:T(8,128)(2,1)S(1)} %get-tuple-element.55.refs_0_, bf16[3072,768]{1,0:T(8,128)(2,1)} %refs_1_.4), custom_call_target="tpu_custom_call" | custom-call | bytes 4718592 | tf_op jit(solution)/shard_map/hold/pallas_call | solution.py:93
  10.1 1.8 %collective-permute-done.1.x_ref = bf16[16,3200]{1,0:T(8,128)(2,1)S(1)} collective-permute-done((bf16[16,3200]{1,0:T(8,128)(2,1)S(1)}, bf16[16,3200]{1,0:T(8,128)(2,1)S(1)}, u32[]{:S(2)}, u32[]{:S(2)}) %collective-permute-start.1) | collective-permute-done | bytes 102432 | tf_op jit(solution)/shard_map/ppermute | solution.py:69
  12.7 3.4 %collective-permute-start.8 = (bf16[2,64,768]{2,1,0:T(8,128)(2,1)S(1)}, bf16[2,64,768]{2,1,0:T(8,128)(2,1)S(1)}, u32[]{:S(2)}, u32[]{:S(2)}) collective-permute-start(bf16[2,64,768]{2,1,0:T(8,128)(2,1)S(1)} %get-tuple-element.67), channel_id=1, source_target_pairs={{0,2},{1,3},{2,0},{3,1},{4,6},{5,7},{6,4},{7,5},{8,10},{9,11},{10,... | collective-permute-start | bytes 589832 | tf_op jit(solution)/shard_map/ppermute | solution.py:69
  19.6 4.0 %collective-permute-start.9 = (bf16[2,64,768]{2,1,0:T(8,128)(2,1)S(1)}, bf16[2,64,768]{2,1,0:T(8,128)(2,1)S(1)}, u32[]{:S(2)}, u32[]{:S(2)}) collective-permute-start(bf16[2,64,768]{2,1,0:T(8,128)(2,1)S(1)} %get-tuple-element.68), channel_id=1, source_target_pairs={{0,3},{1,2},{2,1},{3,0},{4,7},{5,6},{6,5},{7,4},{8,11},{9,10},{10,... | collective-permute-start | bytes 589832 | tf_op jit(solution)/shard_map/ppermute | solution.py:69
  24.8 1.5 %collective-permute-start.6 = (bf16[2,40,384]{2,1,0:T(8,128)(2,1)S(1)}, bf16[2,40,384]{2,1,0:T(8,128)(2,1)S(1)}, u32[]{:S(2)}, u32[]{:S(2)}) collective-permute-start(bf16[2,40,384]{2,1,0:T(8,128)(2,1)S(1)} %join.2.refs_0_), channel_id=1, source_target_pairs={{0,16},{4,20},{8,24},{12,28},{16,0},{20,4},{24,8},{28,12},{1,17},{... | collective-permute-start | bytes 184328 | tf_op jit(solution)/shard_map/ppermute | solution.py:69
  29.1 1.5 %collective-permute-start.7 = (bf16[2,40,384]{2,1,0:T(8,128)(2,1)S(1)}, bf16[2,40,384]{2,1,0:T(8,128)(2,1)S(1)}, u32[]{:S(2)}, u32[]{:S(2)}) collective-permute-start(bf16[2,40,384]{2,1,0:T(8,128)(2,1)S(1)} %collective-permute-done.6.refs_2_), channel_id=1, source_target_pairs={{0,8},{4,12},{8,0},{12,4},{16,24},{20,28},{24,16},{28,20},{1,9},{5... | collective-permute-start | bytes 184328 | tf_op jit(solution)/shard_map/ppermute | solution.py:69
  30.6 2.3 %hold.5 = (bf16[768,3072]{1,0:T(8,128)(2,1)S(1)}, f32[8,128]{1,0:T(8,128)S(1)}) custom-call(f32[8,128]{1,0:T(8,128)S(1)} %get-tuple-element.63.refs_0_.refs_2_, bf16[768,3072]{1,0:T(8,128)(2,1)} %refs_1_.5), custom_call_target="tpu_custom_call" | custom-call | bytes 4718592 | tf_op jit(solution)/shard_map/hold/pallas_call | solution.py:93
  33.3 3.2 %attend.1 = (f32[88,384]{1,0:T(8,128)S(1)}, f32[88,384]{1,0:T(8,128)S(1)}, f32[88,384]{1,0:T(8,128)S(1)}, f32[88,384]{1,0:T(8,128)S(1)}, f32[8,128]{1,0:T(8,128)S(1)}) custom-call(f32[8,128]{1,0:T(8,128)S(1)} %get-tuple-element.64.after_ref, bf16[2,40,384]{2,1,0:T(8,128)(2,1)S(1)} %join.2.refs_0_, bf16[2,40,384]{2,1,0:T(8,128)(2,1)S(1)} %collective-permute-done.5.refs_1_, ...), custom_call_target="tpu_custom_call" | custom-call | tf_op jit(solution)/shard_map/attend/pallas_call | solution.py:334
  36.5 1.5 %collective-permute-start.11 = (f32[88,384]{1,0:T(8,128)S(1)}, f32[88,384]{1,0:T(8,128)S(1)}, u32[]{:S(2)}, u32[]{:S(2)}) collective-permute-start(f32[88,384]{1,0:T(8,128)S(1)} %get-tuple-element.74), channel_id=1, source_target_pairs={{0,8},{4,12},{8,0},{12,4},{16,24},{20,28},{24,16},{28,20},{1,9},{5... | collective-permute-start | bytes 405512 | tf_op jit(solution)/shard_map/ppermute | solution.py:69
  38.1 1.5 %collective-permute-start.12 = (f32[88,384]{1,0:T(8,128)S(1)}, f32[88,384]{1,0:T(8,128)S(1)}, u32[]{:S(2)}, u32[]{:S(2)}) collective-permute-start(f32[88,384]{1,0:T(8,128)S(1)} %get-tuple-element.75), channel_id=1, source_target_pairs={{0,16},{4,20},{8,24},{12,28},{16,0},{20,4},{24,8},{28,12},{1,17},{... | collective-permute-start | bytes 405512 | tf_op jit(solution)/shard_map/ppermute | solution.py:69
  40.0 3.7 %hold.6 = (bf16[3072,1536]{1,0:T(8,128)(2,1)S(1)}, f32[8,128]{1,0:T(8,128)S(1)}) custom-call(f32[8,128]{1,0:T(8,128)S(1)} %get-tuple-element.71.refs_0_, bf16[3072,1536]{1,0:T(8,128)(2,1)} %refs_1_.6), custom_call_target="tpu_custom_call" | custom-call | bytes 9437184 | tf_op jit(solution)/shard_map/hold/pallas_call | solution.py:93
  43.9 1.6 %collective-permute-done.13.refs_3_ = f32[88,384]{1,0:T(8,128)S(1)} collective-permute-done((f32[88,384]{1,0:T(8,128)S(1)}, f32[88,384]{1,0:T(8,128)S(1)}, u32[]{:S(2)}, u32[]{:S(2)}) %collective-permute-start.13) | collective-permute-done | bytes 135200 | tf_op jit(solution)/shard_map/ppermute | solution.py:69
  48.3 1.6 %collective-permute-start.15 = (bf16[80,384]{1,0:T(8,128)(2,1)S(1)}, bf16[80,384]{1,0:T(8,128)(2,1)S(1)}, u32[]{:S(2)}, u32[]{:S(2)}) collective-permute-start(bf16[80,384]{1,0:T(8,128)(2,1)S(1)} %get-tuple-element.84), channel_id=1, source_target_pairs={{0,1},{1,0},{2,3},{3,2},{4,5},{5,4},{6,7},{7,6},{8,9},{9,8},{10,11... | collective-permute-start | bytes 184328 | tf_op jit(solution)/shard_map/ppermute | solution.py:69
  49.9 2.1 %collective-permute-start.16 = (bf16[80,384]{1,0:T(8,128)(2,1)S(1)}, bf16[80,384]{1,0:T(8,128)(2,1)S(1)}, u32[]{:S(2)}, u32[]{:S(2)}) collective-permute-start(bf16[80,384]{1,0:T(8,128)(2,1)S(1)} %get-tuple-element.85), channel_id=1, source_target_pairs={{0,2},{1,3},{2,0},{3,1},{4,6},{5,7},{6,4},{7,5},{8,10},{9,11},{10,... | collective-permute-start | bytes 184328 | tf_op jit(solution)/shard_map/ppermute | solution.py:69
  52.7 3.7 %hold.7 = (bf16[1536,3072]{1,0:T(8,128)(2,1)S(1)}, bf16[64,3072]{1,0:T(8,128)(2,1)S(1)}, f32[8,128]{1,0:T(8,128)S(1)}) custom-call(f32[8,128]{1,0:T(8,128)S(1)} %get-tuple-element.80.refs_0_, bf16[1536,3072]{1,0:T(8,128)(2,1)} %refs_1_.7, bf16[64,3072]{1,0:T(8,128)(2,1)} %refs_2_.1), custom_call_target="tpu_custom_call" | custom-call | bytes 9830400 | tf_op jit(solution)/shard_map/hold/pallas_call | solution.py:93
  62.0 1.7 %collective-permute-done.20.refs_3_ = bf16[80,384]{1,0:T(8,128)(2,1)S(1)} collective-permute-done((bf16[80,384]{1,0:T(8,128)(2,1)S(1)}, bf16[80,384]{1,0:T(8,128)(2,1)S(1)}, u32[]{:S(2)}, u32[]{:S(2)}) %collective-permute-start.20) | collective-permute-done | bytes 61472 | tf_op jit(solution)/shard_map/ppermute | solution.py:69
  65.3 1.5 %collective-permute-done.21.refs_1_ = bf16[4,80,384]{2,1,0:T(8,128)(2,1)S(1)} collective-permute-done((bf16[4,80,384]{2,1,0:T(8,128)(2,1)S(1)}, bf16[4,80,384]{2,1,0:T(8,128)(2,1)S(1)}, u32[]{:S(2)}, u32[]{:S(2)}) %collective-permute-start.21) | collective-permute-done | bytes 245792 | tf_op jit(solution)/shard_map/ppermute | solution.py:69
  66.8 2.7 %mlp.1 = (f32[4,80,384]{2,1,0:T(8,128)S(1)}, bf16[4,80,384]{2,1,0:T(8,128)(2,1)S(1)}) custom-call(bf16[4,80,384]{2,1,0:T(8,128)(2,1)S(1)} %join.3.refs_0_, bf16[4,80,384]{2,1,0:T(8,128)(2,1)S(1)} %collective-permute-done.21.refs_1_, bf16[3072,1536]{1,0:T(8,128)(2,1)S(1)} %get-tuple-element.89.refs_2_, bf16[1536,3072]{1,0:T(8,128)(2,1)S(1)} %get-tuple-element.90.refs_3_), custom_call_target="tpu_custom_call" | custom-call | tf_op jit(solution)/shard_map/mlp/pallas_call | solution.py:456
  76.4 2.3 %collective-permute-done.25.refs_3_ = bf16[80,384]{1,0:T(8,128)(2,1)S(1)} collective-permute-done((bf16[80,384]{1,0:T(8,128)(2,1)S(1)}, bf16[80,384]{1,0:T(8,128)(2,1)S(1)}, u32[]{:S(2)}, u32[]{:S(2)}) %collective-permute-start.25) | collective-permute-done | bytes 61472 | tf_op jit(solution)/shard_map/ppermute | solution.py:69
  78.8 1.8 %collective-permute-start.28 = (bf16[16,384]{1,0:T(8,128)(2,1)S(1)}, bf16[16,384]{1,0:T(8,128)(2,1)S(1)}, u32[]{:S(2)}, u32[]{:S(2)}) collective-permute-start(bf16[16,384]{1,0:T(8,128)(2,1)S(1)} %get-tuple-element.98.refs_0_), channel_id=1, source_target_pairs={{0,3},{1,2},{2,1},{3,0},{4,7},{5,6},{6,5},{7,4},{8,11},{9,10},{10,... | collective-permute-start | bytes 36872 | tf_op jit(solution)/shard_map/ppermute | solution.py:69
  80.9 2.3 %collective-permute-start.26 = (bf16[16,384]{1,0:T(8,128)(2,1)S(1)}, bf16[16,384]{1,0:T(8,128)(2,1)S(1)}, u32[]{:S(2)}, u32[]{:S(2)}) collective-permute-start(bf16[16,384]{1,0:T(8,128)(2,1)S(1)} %get-tuple-element.98.refs_0_), channel_id=1, source_target_pairs={{0,1},{1,0},{2,3},{3,2},{4,5},{5,4},{6,7},{7,6},{8,9},{9,8},{10,11... | collective-permute-start | bytes 36872 | tf_op jit(solution)/shard_map/ppermute | solution.py:69
  (55 shorter events, 30.5 us)
Async XLA Ops:
  2.0 10.7 %collective-permute-start = (bf16[4,64,768]{2,1,0:T(8,128)(2,1)S(1)}, bf16[4,64,768]{2,1,0:T(8,128)(2,1)S(1)}, u32[]{:S(2)}, u32[]{:S(2)}) collective-permute-start(bf16[4,64,768]{2,1,0:T(8,128)(2,1)S(1)} %get-tuple-element.54), channel_id=1, source_target_pairs={{0,4},{4,0},{8,12},{12,8},{16,20},{20,16},{24,28},{28,24},{1,5},{5... | collective-permute-start | bytes 1179656 | tf_op jit(solution)/shard_map/ppermute | solution.py:69
  2.6 9.4 %collective-permute-start.1 = (bf16[16,3200]{1,0:T(8,128)(2,1)S(1)}, bf16[16,3200]{1,0:T(8,128)(2,1)S(1)}, u32[]{:S(2)}, u32[]{:S(2)}) collective-permute-start(bf16[16,3200]{1,0:T(8,128)(2,1)S(1)} %get-tuple-element.55.refs_0_), channel_id=1, source_target_pairs={{0,2},{1,3},{2,0},{3,1},{4,6},{5,7},{6,4},{7,5},{8,10},{9,11},{10,... | collective-permute-start | bytes 307208 | tf_op jit(solution)/shard_map/ppermute | solution.py:69
  6.2 10.0 %collective-permute-start.2 = (bf16[16,3200]{1,0:T(8,128)(2,1)S(1)}, bf16[16,3200]{1,0:T(8,128)(2,1)S(1)}, u32[]{:S(2)}, u32[]{:S(2)}) collective-permute-start(bf16[16,3200]{1,0:T(8,128)(2,1)S(1)} %get-tuple-element.55.refs_0_), channel_id=1, source_target_pairs={{0,1},{1,0},{2,3},{3,2},{4,5},{5,4},{6,7},{7,6},{8,9},{9,8},{10,11... | collective-permute-start | bytes 307208 | tf_op jit(solution)/shard_map/ppermute | solution.py:69
  12.0 4.7 %collective-permute-start.3 = (bf16[16,3200]{1,0:T(8,128)(2,1)S(1)}, bf16[16,3200]{1,0:T(8,128)(2,1)S(1)}, u32[]{:S(2)}, u32[]{:S(2)}) collective-permute-start(bf16[16,3200]{1,0:T(8,128)(2,1)S(1)} %relay.1.refs_2_.refs_4_), channel_id=1, source_target_pairs={{0,1},{1,0},{2,3},{3,2},{4,5},{5,4},{6,7},{7,6},{8,9},{9,8},{10,11... | collective-permute-start | bytes 307208 | tf_op jit(solution)/shard_map/ppermute | solution.py:69
  12.7 20.5 %collective-permute-start.8 = (bf16[2,64,768]{2,1,0:T(8,128)(2,1)S(1)}, bf16[2,64,768]{2,1,0:T(8,128)(2,1)S(1)}, u32[]{:S(2)}, u32[]{:S(2)}) collective-permute-start(bf16[2,64,768]{2,1,0:T(8,128)(2,1)S(1)} %get-tuple-element.67), channel_id=1, source_target_pairs={{0,2},{1,3},{2,0},{3,1},{4,6},{5,7},{6,4},{7,5},{8,10},{9,11},{10,... | collective-permute-start | bytes 589832 | tf_op jit(solution)/shard_map/ppermute | solution.py:69
  18.8 14.5 %collective-permute-start.10 = (bf16[2,64,768]{2,1,0:T(8,128)(2,1)S(1)}, bf16[2,64,768]{2,1,0:T(8,128)(2,1)S(1)}, u32[]{:S(2)}, u32[]{:S(2)}) collective-permute-start(bf16[2,64,768]{2,1,0:T(8,128)(2,1)S(1)} %get-tuple-element.70), channel_id=1, source_target_pairs={{0,1},{1,0},{2,3},{3,2},{4,5},{5,4},{6,7},{7,6},{8,9},{9,8},{10,11... | collective-permute-start | bytes 589832 | tf_op jit(solution)/shard_map/ppermute | solution.py:69
  19.6 13.7 %collective-permute-start.9 = (bf16[2,64,768]{2,1,0:T(8,128)(2,1)S(1)}, bf16[2,64,768]{2,1,0:T(8,128)(2,1)S(1)}, u32[]{:S(2)}, u32[]{:S(2)}) collective-permute-start(bf16[2,64,768]{2,1,0:T(8,128)(2,1)S(1)} %get-tuple-element.68), channel_id=1, source_target_pairs={{0,3},{1,2},{2,1},{3,0},{4,7},{5,6},{6,5},{7,4},{8,11},{9,10},{10,... | collective-permute-start | bytes 589832 | tf_op jit(solution)/shard_map/ppermute | solution.py:69
  24.8 4.2 %collective-permute-start.6 = (bf16[2,40,384]{2,1,0:T(8,128)(2,1)S(1)}, bf16[2,40,384]{2,1,0:T(8,128)(2,1)S(1)}, u32[]{:S(2)}, u32[]{:S(2)}) collective-permute-start(bf16[2,40,384]{2,1,0:T(8,128)(2,1)S(1)} %join.2.refs_0_), channel_id=1, source_target_pairs={{0,16},{4,20},{8,24},{12,28},{16,0},{20,4},{24,8},{28,12},{1,17},{... | collective-permute-start | bytes 184328 | tf_op jit(solution)/shard_map/ppermute | solution.py:69
  26.4 6.6 %collective-permute-start.5 = (bf16[2,40,384]{2,1,0:T(8,128)(2,1)S(1)}, bf16[2,40,384]{2,1,0:T(8,128)(2,1)S(1)}, u32[]{:S(2)}, u32[]{:S(2)}) collective-permute-start(bf16[2,40,384]{2,1,0:T(8,128)(2,1)S(1)} %join.2.refs_0_), channel_id=1, source_target_pairs={{0,8},{4,12},{8,0},{12,4},{16,24},{20,28},{24,16},{28,20},{1,9},{5... | collective-permute-start | bytes 184328 | tf_op jit(solution)/shard_map/ppermute | solution.py:69
  29.1 4.2 %collective-permute-start.7 = (bf16[2,40,384]{2,1,0:T(8,128)(2,1)S(1)}, bf16[2,40,384]{2,1,0:T(8,128)(2,1)S(1)}, u32[]{:S(2)}, u32[]{:S(2)}) collective-permute-start(bf16[2,40,384]{2,1,0:T(8,128)(2,1)S(1)} %collective-permute-done.6.refs_2_), channel_id=1, source_target_pairs={{0,8},{4,12},{8,0},{12,4},{16,24},{20,28},{24,16},{28,20},{1,9},{5... | collective-permute-start | bytes 184328 | tf_op jit(solution)/shard_map/ppermute | solution.py:69
  36.5 7.2 %collective-permute-start.11 = (f32[88,384]{1,0:T(8,128)S(1)}, f32[88,384]{1,0:T(8,128)S(1)}, u32[]{:S(2)}, u32[]{:S(2)}) collective-permute-start(f32[88,384]{1,0:T(8,128)S(1)} %get-tuple-element.74), channel_id=1, source_target_pairs={{0,8},{4,12},{8,0},{12,4},{16,24},{20,28},{24,16},{28,20},{1,9},{5... | collective-permute-start | bytes 405512 | tf_op jit(solution)/shard_map/ppermute | solution.py:69
  38.1 5.8 %collective-permute-start.12 = (f32[88,384]{1,0:T(8,128)S(1)}, f32[88,384]{1,0:T(8,128)S(1)}, u32[]{:S(2)}, u32[]{:S(2)}) collective-permute-start(f32[88,384]{1,0:T(8,128)S(1)} %get-tuple-element.75), channel_id=1, source_target_pairs={{0,16},{4,20},{8,24},{12,28},{16,0},{20,4},{24,8},{28,12},{1,17},{... | collective-permute-start | bytes 405512 | tf_op jit(solution)/shard_map/ppermute | solution.py:69
  39.6 5.9 %collective-permute-start.13 = (f32[88,384]{1,0:T(8,128)S(1)}, f32[88,384]{1,0:T(8,128)S(1)}, u32[]{:S(2)}, u32[]{:S(2)}) collective-permute-start(f32[88,384]{1,0:T(8,128)S(1)} %get-tuple-element.76), channel_id=1, source_target_pairs={{0,24},{4,28},{8,16},{12,20},{16,8},{20,12},{24,0},{28,4},{1,25},{... | collective-permute-start | bytes 405512 | tf_op jit(solution)/shard_map/ppermute | solution.py:69
  48.3 8.2 %collective-permute-start.15 = (bf16[80,384]{1,0:T(8,128)(2,1)S(1)}, bf16[80,384]{1,0:T(8,128)(2,1)S(1)}, u32[]{:S(2)}, u32[]{:S(2)}) collective-permute-start(bf16[80,384]{1,0:T(8,128)(2,1)S(1)} %get-tuple-element.84), channel_id=1, source_target_pairs={{0,1},{1,0},{2,3},{3,2},{4,5},{5,4},{6,7},{7,6},{8,9},{9,8},{10,11... | collective-permute-start | bytes 184328 | tf_op jit(solution)/shard_map/ppermute | solution.py:69
  49.9 7.3 %collective-permute-start.16 = (bf16[80,384]{1,0:T(8,128)(2,1)S(1)}, bf16[80,384]{1,0:T(8,128)(2,1)S(1)}, u32[]{:S(2)}, u32[]{:S(2)}) collective-permute-start(bf16[80,384]{1,0:T(8,128)(2,1)S(1)} %get-tuple-element.85), channel_id=1, source_target_pairs={{0,2},{1,3},{2,0},{3,1},{4,6},{5,7},{6,4},{7,5},{8,10},{9,11},{10,... | collective-permute-start | bytes 184328 | tf_op jit(solution)/shard_map/ppermute | solution.py:69
  52.0 6.1 %collective-permute-start.17 = (bf16[80,384]{1,0:T(8,128)(2,1)S(1)}, bf16[80,384]{1,0:T(8,128)(2,1)S(1)}, u32[]{:S(2)}, u32[]{:S(2)}) collective-permute-start(bf16[80,384]{1,0:T(8,128)(2,1)S(1)} %get-tuple-element.86), channel_id=1, source_target_pairs={{0,3},{1,2},{2,1},{3,0},{4,7},{5,6},{6,5},{7,4},{8,11},{9,10},{10,... | collective-permute-start | bytes 184328 | tf_op jit(solution)/shard_map/ppermute | solution.py:69
  58.4 5.2 %collective-permute-start.20 = (bf16[80,384]{1,0:T(8,128)(2,1)S(1)}, bf16[80,384]{1,0:T(8,128)(2,1)S(1)}, u32[]{:S(2)}, u32[]{:S(2)}) collective-permute-start(bf16[80,384]{1,0:T(8,128)(2,1)S(1)} %get-tuple-element.88.refs_0_), channel_id=1, source_target_pairs={{0,24},{4,28},{8,16},{12,20},{16,8},{20,12},{24,0},{28,4},{1,25},{... | collective-permute-start | bytes 184328 | tf_op jit(solution)/shard_map/ppermute | solution.py:69
  59.7 4.5 %collective-permute-start.19 = (bf16[80,384]{1,0:T(8,128)(2,1)S(1)}, bf16[80,384]{1,0:T(8,128)(2,1)S(1)}, u32[]{:S(2)}, u32[]{:S(2)}) collective-permute-start(bf16[80,384]{1,0:T(8,128)(2,1)S(1)} %get-tuple-element.88.refs_0_), channel_id=1, source_target_pairs={{0,16},{4,20},{8,24},{12,28},{16,0},{20,4},{24,8},{28,12},{1,17},{... | collective-permute-start | bytes 184328 | tf_op jit(solution)/shard_map/ppermute | solution.py:69
  60.9 4.2 %collective-permute-start.18 = (bf16[80,384]{1,0:T(8,128)(2,1)S(1)}, bf16[80,384]{1,0:T(8,128)(2,1)S(1)}, u32[]{:S(2)}, u32[]{:S(2)}) collective-permute-start(bf16[80,384]{1,0:T(8,128)(2,1)S(1)} %get-tuple-element.88.refs_0_), channel_id=1, source_target_pairs={{0,8},{4,12},{8,0},{12,4},{16,24},{20,28},{24,16},{28,20},{1,9},{5... | collective-permute-start | bytes 184328 | tf_op jit(solution)/shard_map/ppermute | solution.py:69
  71.1 4.3 %collective-permute-start.23 = (bf16[80,384]{1,0:T(8,128)(2,1)S(1)}, bf16[80,384]{1,0:T(8,128)(2,1)S(1)}, u32[]{:S(2)}, u32[]{:S(2)}) collective-permute-start(bf16[80,384]{1,0:T(8,128)(2,1)S(1)} %get-tuple-element.94), channel_id=1, source_target_pairs={{0,8},{4,12},{8,0},{12,4},{16,24},{20,28},{24,16},{28,20},{1,9},{5... | collective-permute-start | bytes 184328 | tf_op jit(solution)/shard_map/ppermute | solution.py:69
  73.6 5.1 %collective-permute-start.25 = (bf16[80,384]{1,0:T(8,128)(2,1)S(1)}, bf16[80,384]{1,0:T(8,128)(2,1)S(1)}, u32[]{:S(2)}, u32[]{:S(2)}) collective-permute-start(bf16[80,384]{1,0:T(8,128)(2,1)S(1)} %get-tuple-element.96), channel_id=1, source_target_pairs={{0,24},{4,28},{8,16},{12,20},{16,8},{20,12},{24,0},{28,4},{1,25},{... | collective-permute-start | bytes 184328 | tf_op jit(solution)/shard_map/ppermute | solution.py:69
  78.8 5.6 %collective-permute-start.28 = (bf16[16,384]{1,0:T(8,128)(2,1)S(1)}, bf16[16,384]{1,0:T(8,128)(2,1)S(1)}, u32[]{:S(2)}, u32[]{:S(2)}) collective-permute-start(bf16[16,384]{1,0:T(8,128)(2,1)S(1)} %get-tuple-element.98.refs_0_), channel_id=1, source_target_pairs={{0,3},{1,2},{2,1},{3,0},{4,7},{5,6},{6,5},{7,4},{8,11},{9,10},{10,... | collective-permute-start | bytes 36872 | tf_op jit(solution)/shard_map/ppermute | solution.py:69
  80.6 4.6 %collective-permute-start.27 = (bf16[16,384]{1,0:T(8,128)(2,1)S(1)}, bf16[16,384]{1,0:T(8,128)(2,1)S(1)}, u32[]{:S(2)}, u32[]{:S(2)}) collective-permute-start(bf16[16,384]{1,0:T(8,128)(2,1)S(1)} %get-tuple-element.98.refs_0_), channel_id=1, source_target_pairs={{0,2},{1,3},{2,0},{3,1},{4,6},{5,7},{6,4},{7,5},{8,10},{9,11},{10,... | collective-permute-start | bytes 36872 | tf_op jit(solution)/shard_map/ppermute | solution.py:69
  80.9 4.3 %collective-permute-start.26 = (bf16[16,384]{1,0:T(8,128)(2,1)S(1)}, bf16[16,384]{1,0:T(8,128)(2,1)S(1)}, u32[]{:S(2)}, u32[]{:S(2)}) collective-permute-start(bf16[16,384]{1,0:T(8,128)(2,1)S(1)} %get-tuple-element.98.refs_0_), channel_id=1, source_target_pairs={{0,1},{1,0},{2,3},{3,2},{4,5},{5,4},{6,7},{7,6},{8,9},{9,8},{10,11... | collective-permute-start | bytes 36872 | tf_op jit(solution)/shard_map/ppermute | solution.py:69
  (5 other events, 9.9 us)
